TPU v7x, 32 devices: a whole 2x2x4 slice. The times are simulated.
32 devices in a mesh: groups: 2 (over x), pool: 8 (over z, y), section: 2 (over core).
Axes of the slice: x: 2, y: 2, z: 4, core: 2. Of those that a mesh axis runs over, the one named last changes fastest.
Arguments:
- x_gate: bfloat16 [2, 16, 128, 16384], P('section', ('groups', 'pool')), parts along dimension 1, may hold values from -6 to 6
- dt_raw: bfloat16 [2, 16, 128, 8192], P('section', ('groups', 'pool')), parts along dimension 1, may hold values from -2 to 8
- state_maps: bfloat16 [2, 16, 128, 32], P('section', ('groups', 'pool')), parts along dimension 1, may hold values from -6 to 6
- a_log: float32 [2, 16, 8192], P('section'), may hold values from 0 to 2.77
- conv_weight: float32 [2, 4, 8192], P('section'), may hold values from -3 to 3
- dt_bias: float32 [2, 8192], P('section'), may hold values from -8.6 to -2.4
- d_skip: float32 [2, 8192], P('section'), may hold values from 0.1 to 1.9
- state_pool: float32 [2, 32, 16, 8192], P('section', ('groups', 'pool')), parts along dimension 1, may hold values from -6 to 6
- conv_pool: bfloat16 [2, 32, 3, 8192], P('section', ('groups', 'pool')), parts along dimension 1, may hold values from -6 to 6
- queries: bfloat16 [2, 16, 128, 2048], P('section', ('groups', 'pool')), parts along dimension 1, may hold values from -18 to 18
- suffix_kv: bfloat16 [2, 16, 128, 1024], P('section', ('groups', 'pool')), parts along dimension 1, may hold values from -6 to 6
- kv_pool: bfloat16 [2, 128, 64, 1024], P('section', ('groups', 'pool')), parts along dimension 1, may hold values from -10.5 to 10.5
- state_slot: int32 [2, 16], P('section', ('groups', 'pool')), parts along dimension 1, may hold values from 0 to 15, as said below
- kv_ids: int32 [2, 16, 8], P('section', ('groups', 'pool')), parts along dimension 1, may hold values from 0 to 63, as said below
- prefix_blocks: int32 [2, 16], P('section', ('groups', 'pool')), parts along dimension 1, may hold values from 1 to 8, as said below
Outputs:
- mamba_out: bfloat16 [2, 16, 128, 8192], P('section', ('groups', 'pool')), parts along dimension 1
- final_state: float32 [2, 16, 16, 8192], P('section', ('groups', 'pool')), parts along dimension 1
- attn_out: bfloat16 [2, 16, 128, 2048], P('section', ('groups', 'pool')), parts along dimension 1
There are 2 independent parts, one for each index of `groups`. A program takes and returns all parts, laid end to end along the dimension named above; an argument that names none is the same for every part. Nothing has to cross between parts.
Inputs may be any that keep to these rules, and one draw needn't show every extreme that they name: `state_slot`: slot s of owner o is o * 2 + s; over the requests of a layer at most 1 distinct slots of one owner are named, and some owner has exactly 1. `kv_ids`: block b of owner o is o * 8 + b; a request's entries are distinct and all name cached blocks, those past its prefix too; over all entries of a layer at most 4 distinct blocks of one owner are named, and some owner has exactly 4. `prefix_blocks`: some request of each layer has 8.
All inputs are finite; a program needn't handle non-finite values.
Results may differ from a plain program's by a relative error of at most 0.0049.
Values may be sent and summed in bfloat16 or wider, within the bound.
A program may use at most 128 MiB of HBM per device.

v0:
```python
import math

import jax
import jax.numpy as jnp
from jax import lax
from jax.sharding import PartitionSpec as P

DI = 8192
NS = 16
KW = 4
HD = 128
HQ = 16
HK = 4
NEW_TOKENS = 128
BLK = 64
KVW = 1024


def mixer(x_gate, dt_raw, state_maps, start_state, conv_state, a_log, conv_weight, dt_bias, d_skip):
    inputs_part = x_gate[:, :DI].astype(jnp.float32)
    gate_part = x_gate[:, DI:].astype(jnp.float32)
    padded = jnp.concatenate([conv_state.astype(jnp.float32), inputs_part], axis=0)
    convolved = conv_weight[0][None, :] * padded[0:NEW_TOKENS]
    for offset in range(1, KW):
        convolved = convolved + conv_weight[offset][None, :] * padded[offset : offset + NEW_TOKENS]
    signal = jax.nn.silu(convolved)
    step_rate = jax.nn.softplus(dt_raw.astype(jnp.float32) + dt_bias[None, :])
    decay_coef = -jnp.exp(a_log)
    b_part = state_maps[:, :NS].astype(jnp.float32)
    c_part = state_maps[:, NS:].astype(jnp.float32)
    span = 8
    block_count = NEW_TOKENS // span
    rate_blocks = step_rate.reshape(block_count, span, DI)
    signal_blocks = signal.reshape(block_count, span, DI)
    b_blocks = b_part.reshape(block_count, span, NS)
    c_blocks = c_part.reshape(block_count, span, NS)

    def advance_block(ssm_state, inputs):
        rate_rows, signal_rows, b_rows, c_rows = inputs
        produced = []
        for inner in range(span):
            rate_now = rate_rows[inner]
            ssm_state = (
                jnp.exp(rate_now[None, :] * decay_coef) * ssm_state
                + (rate_now * signal_rows[inner])[None, :] * b_rows[inner][:, None]
            )
            produced.append(jnp.sum(c_rows[inner][:, None] * ssm_state, axis=0))
        return (ssm_state, jnp.stack(produced))

    last_state, outputs = lax.scan(
        advance_block, start_state, (rate_blocks, signal_blocks, b_blocks, c_blocks)
    )
    outputs = outputs.reshape(NEW_TOKENS, DI)
    result = ((outputs + d_skip[None, :] * signal) * jax.nn.silu(gate_part)).astype(jnp.bfloat16)
    return (result, last_state)


def attend(queries, suffix_kv, blocks, used_blocks):
    prefix_rows = blocks.shape[0] * BLK
    key_count = prefix_rows + NEW_TOKENS
    group_size = HQ // HK
    score_scale = 1.0 / math.sqrt(HD)
    keys_all = jnp.concatenate([blocks.reshape(prefix_rows, KVW), suffix_kv], axis=0)
    key_heads = keys_all[:, : HK * HD].reshape(key_count, HK, HD)
    value_heads = keys_all[:, HK * HD :].reshape(key_count, HK, HD)
    query_heads = queries.reshape(NEW_TOKENS, HK, group_size, HD)
    scores = (
        jnp.einsum("tkgd,skd->kgts", query_heads, key_heads, preferred_element_type=jnp.float32)
        * score_scale
    )
    positions = jnp.arange(key_count, dtype=jnp.int32)[None, :]
    query_rows = jnp.arange(NEW_TOKENS, dtype=jnp.int32)[:, None]
    allowed = jnp.where(
        positions < prefix_rows,
        positions < used_blocks * BLK,
        positions - prefix_rows <= query_rows,
    )
    scores = jnp.where(allowed[None, None], scores, -1e30)
    row_max = jnp.max(scores, axis=-1, keepdims=True)
    weights = jnp.exp(scores - row_max)
    probs = (weights / jnp.sum(weights, axis=-1, keepdims=True)).astype(jnp.bfloat16)
    mixed = jnp.einsum("kgts,skd->tkgd", probs, value_heads, preferred_element_type=jnp.float32)
    return mixed.reshape(NEW_TOKENS, HQ * HD).astype(jnp.bfloat16)


def on_device(
    x_gate,
    dt_raw,
    state_maps,
    a_log,
    conv_weight,
    dt_bias,
    d_skip,
    state_pool,
    conv_pool,
    queries,
    suffix_kv,
    kv_pool,
    state_slot,
    kv_ids,
    prefix_blocks,
):
    owners = lax.axis_size("pool")
    slots_here = state_pool.shape[1]
    blocks_here = kv_pool.shape[1]
    prefix_len = kv_ids.shape[2]
    state_piece = NS * DI // owners
    conv_piece = (KW - 1) * DI // owners
    block_piece = BLK * KVW // owners
    all_slots, all_blocks = (
        lax.all_gather(state_slot[0], "pool", axis=0, tiled=True),
        lax.all_gather(kv_ids[0], "pool", axis=0, tiled=True),
    )
    state_rows = state_pool[0].reshape(slots_here, owners, state_piece)
    conv_rows = conv_pool[0].reshape(slots_here, owners, conv_piece)
    block_rows = kv_pool[0].reshape(blocks_here, owners, block_piece)
    held_state = lax.all_to_all(state_rows, "pool", split_axis=1, concat_axis=0, tiled=True)
    held_conv, held_blocks = (
        lax.all_to_all(conv_rows, "pool", split_axis=1, concat_axis=0, tiled=True),
        lax.all_to_all(block_rows, "pool", split_axis=1, concat_axis=0, tiled=True),
    )
    send_state = held_state.reshape(-1, state_piece)[all_slots].reshape(owners, 1, 1, state_piece)
    send_conv = held_conv.reshape(-1, conv_piece)[all_slots].reshape(owners, 1, 1, conv_piece)
    send_blocks = held_blocks.reshape(-1, block_piece)[all_blocks].reshape(
        owners, prefix_len, 1, block_piece
    )
    start_state = lax.all_to_all(
        send_state, "pool", split_axis=0, concat_axis=2, tiled=True
    ).reshape(NS, DI)
    conv_state, blocks = (
        lax.all_to_all(send_conv, "pool", split_axis=0, concat_axis=2, tiled=True),
        lax.all_to_all(send_blocks, "pool", split_axis=0, concat_axis=2, tiled=True),
    )
    conv_state = conv_state.reshape(KW - 1, DI)
    blocks = blocks.reshape(prefix_len, BLK, KVW)
    mixed_out, last_state = mixer(
        x_gate[0, 0],
        dt_raw[0, 0],
        state_maps[0, 0],
        start_state,
        conv_state,
        a_log[0],
        conv_weight[0],
        dt_bias[0],
        d_skip[0],
    )
    attended = attend(queries[0, 0], suffix_kv[0, 0], blocks, prefix_blocks[0, 0])
    return (mixed_out[None, None], last_state[None, None], attended[None, None])


def solution(mesh):
    placed = (
        P("section", ("groups", "pool"), None, None),
        P("section", ("groups", "pool"), None, None),
        P("section", ("groups", "pool"), None, None),
        P("section", None, None),
        P("section", None, None),
        P("section", None),
        P("section", None),
        P("section", ("groups", "pool"), None, None),
        P("section", ("groups", "pool"), None, None),
        P("section", ("groups", "pool"), None, None),
        P("section", ("groups", "pool"), None, None),
        P("section", ("groups", "pool"), None, None),
        P("section", ("groups", "pool")),
        P("section", ("groups", "pool"), None),
        P("section", ("groups", "pool")),
    )
    return jax.shard_map(
        on_device,
        mesh=mesh,
        in_specs=placed,
        out_specs=(
            P("section", ("groups", "pool"), None, None),
            P("section", ("groups", "pool"), None, None),
            P("section", ("groups", "pool"), None, None),
        ),
        check_vma=False,
    )
```

profile of v0, /device:TPU:14, one launch (start us, length us, event | category | flops | bytes accessed | tf_op | source)
XLA Modules:
  0.0 264.9 jit_solution(5388771456560183827)
XLA Ops:
  0.7 6.4 %all-to-all-start.2 = ((bf16[2,8,3072]{2,0,1:T(2,128)(2,1)}), bf16[2,8,3072]{2,0,1:T(2,128)(2,1)S(1)}, u32[]{:S(2)}, u32[]{:S(2)}) async-start(bf16[2,8,3072]{2,0,1:T(2,128)(2,1)} %bitcast.291), calls=%async_computation.2 | async-start | bytes 196608 | tf_op jit(solution)/shard_map/all_to_all | solution.py:119
  7.7 1.2 dynamic-slice
  9.6 10.4 %all-reduce = s32[8]{0:T(128)S(1)} all-reduce(s32[8]{0:T(128)S(1)} %bitcast_dynamic-update-slice_fusion.1), channel_id=2, replica_groups=mesh['groups'=2,'pool'=8,'section'=2] {'pool'}, use_global_device_ids=true, to_apply=%add | all-reduce | flops 8 | bytes 64 | tf_op jit(solution)/shard_map/all_gather | solution.py:111
  20.0 4.0 %slice_convert_fusion = f32[128,8192]{1,0:T(8,128)} fusion(bf16[128,16384]{1,0:T(8,128)(2,1)} %bitcast.258), kind=kLoop, calls=%fused_computation.93 | loop fusion | flops 1048576 | bytes 6291456 | tf_op jit(solution)/shard_map/convert_element_type | solution.py:20
  24.8 15.0 %all-gather.1 = s32[8,1,8]{2,1,0:T(1,128)S(1)} all-gather(s32[1,1,8]{2,1,0:T(1,128)S(1)} %copy-done.12), channel_id=3, replica_groups=mesh['groups'=2,'pool'=8,'section'=2] {'pool'}, dimensions={0}, use_global_device_ids=true | all-gather | bytes 288 | tf_op jit(solution)/shard_map/all_gather | solution.py:112
  39.7 4.4 %compare_select_fusion = f32[16,8,8192]{2,1,0:T(8,128)} fusion(bf16[1,1,128,8192]{3,2,1,0:T(8,128)(2,1)S(1)} %copy-done.2, f32[8192]{0:T(1024)S(1)} %bitcast.292), kind=kLoop, calls=%fused_computation.55 | loop fusion | flops 8388608 | bytes 6324224 | tf_op jit(solution)/shard_map/jit(softplus)/select_n | solution.py:27
  44.1 1.0 fusion.30
  47.5 7.4 %all-to-all-start.3 = ((bf16[8,2,1536]{2,1,0:T(2,128)(2,1)}), bf16[8,2,1536]{2,1,0:T(2,128)(2,1)S(1)}, u32[]{:S(2)}, u32[]{:S(2)}) async-start(bf16[8,2,1536]{2,1,0:T(2,128)(2,1)} %reshape.389), calls=%async_computation.3 | async-start | bytes 98304 | tf_op jit(solution)/shard_map/all_to_all | solution.py:131
  55.3 1.8 copy.39
  57.2 2.4 all-to-all-done.3
  59.5 5.8 %all-to-all-start = ((f32[2,8,16384]{2,0,1:T(2,128)}), f32[2,8,16384]{2,0,1:T(2,128)S(1)}, u32[]{:S(2)}, u32[]{:S(2)}) async-start(f32[2,8,16384]{2,0,1:T(2,128)} %copy.39), calls=%async_computation | async-start | bytes 2097152 | tf_op jit(solution)/shard_map/all_to_all | solution.py:117
  66.8 1.6 reshape_squeeze.14
  68.4 1.6 copy.44
  70.0 1.2 reshape_squeeze.15
  71.2 8.7 %all-to-all-done = f32[2,8,16384]{2,0,1:T(2,128)S(1)} async-done(((f32[2,8,16384]{2,0,1:T(2,128)}), f32[2,8,16384]{2,0,1:T(2,128)S(1)}, u32[]{:S(2)}, u32[]{:S(2)}) %all-to-all-start) | async-done | bytes 1048608 | tf_op jit(solution)/shard_map/all_to_all | solution.py:117
  79.9 7.2 %all-to-all-start.4 = ((bf16[8,8,8192]{2,0,1:T(8,128)(2,1)}), bf16[8,8,8192]{2,0,1:T(8,128)(2,1)S(1)}, u32[]{:S(2)}, u32[]{:S(2)}) async-start(bf16[8,8,8192]{2,0,1:T(8,128)(2,1)} %copy.44), calls=%async_computation.4 | async-start | bytes 2097152 | tf_op jit(solution)/shard_map/all_to_all | solution.py:120
  87.6 1.9 reshape.325
  90.3 1.3 copy.40
  91.6 14.7 %all-to-all-done.4 = bf16[8,8,8192]{2,0,1:T(8,128)(2,1)S(1)} async-done(((bf16[8,8,8192]{2,0,1:T(8,128)(2,1)}), bf16[8,8,8192]{2,0,1:T(8,128)(2,1)S(1)}, u32[]{:S(2)}, u32[]{:S(2)}) %all-to-all-start.4) | async-done | bytes 1048608 | tf_op jit(solution)/shard_map/all_to_all | solution.py:120
  106.3 6.9 %all-to-all-start.1 = ((f32[8,1,1,16384]{3,2,1,0:T(1,128)}), f32[8,1,1,16384]{3,2,1,0:T(1,128)S(1)}, u32[]{:S(2)}, u32[]{:S(2)}) async-start(f32[8,1,1,16384]{3,2,1,0:T(1,128)} %copy.40), calls=%async_computation.1 | async-start | bytes 1048576 | tf_op jit(solution)/shard_map/all_to_all | solution.py:127
  113.2 8.9 %divide_multiply_fusion = f32[128,8192]{1,0:T(8,128)} fusion(f32[128,8192]{1,0:T(8,128)} %slice_convert_fusion, f32[3,8192]{1,0:T(4,128)S(1)} %reshape.341, f32[8192]{0:T(1024)S(1)} %bitcast.287, f32[8192]{0:T(1024)S(1)} %bitcast.288, f32[8192]{0:T(1024)S(1)} %bitcast.286, f32[8192]{0:T(1024)S(1)} %bitcast.285), kind=kLoop, calls=%fused_computation.86 | loop fusion | flops 14680064 | bytes 8617984 | tf_op jit(solution)/shard_map/jit(silu)/mul | solution.py:26
  122.1 2.3 gather_fusion.2
  124.4 6.0 %all-to-all-start.5 = ((bf16[8,8,1,8192]{3,1,2,0:T(8,128)(2,1)}), bf16[8,8,1,8192]{3,1,2,0:T(8,128)(2,1)S(1)}, u32[]{:S(2)}, u32[]{:S(2)}) async-start(bf16[8,8,1,8192]{3,1,2,0:T(8,128)(2,1)} %bitcast.71), calls=%async_computation.5 | async-start | bytes 2097152 | tf_op jit(solution)/shard_map/all_to_all | solution.py:132
  130.4 1.2 reduce
  131.7 118.4 %while.13 = (s32[]{:T(128)}, f32[16,8192]{1,0:T(8,128)S(1)}, f32[16,8,8192]{2,1,0:T(8,128)}, f32[16,8,8192]{2,1,0:T(8,128)}, f32[16,8192]{1,0:T(8,128)S(1)}, /*i...) while((s32[]{:T(128)}, f32[16,8192]{1,0:T(8,128)S(1)}, ...), condition=%wide.region_9.10_spmd.clone, body=%wide.region_0.9_spmd.sunk.clone | while | flops 9437193 | bytes 8263757 | solution.py:50
  131.7 3.1 %constant_dynamic-slice_fusion.23 = (f32[1,1,8192]{2,1,0:T(1,128)S(1)}, f32[1,1,8192]{2,1,0:T(1,128)S(1)}, f32[1,1,8192]{2,1,0:T(1,128)S(1)}, f32[1,1,8192]{2,1,...) fusion(f32[16,8,8192]{2,1,0:T(8,128)} %get-tuple-element.365, ...), kind=kLoop, calls=%fused_computation.26.clone.1.clone | loop fusion | bytes 1048608 | tf_op jit(solution)/shard_map/while/body/eval_jaxpr/slice | solution.py:45
  136.3 1.1 multiply_reduce_fusion.14
  139.2 2.8 %constant_dynamic-slice_fusion.23 = (f32[1,1,8192]{2,1,0:T(1,128)S(1)}, f32[1,1,8192]{2,1,0:T(1,128)S(1)}, f32[1,1,8192]{2,1,0:T(1,128)S(1)}, f32[1,1,8192]{2,1,...) fusion(f32[16,8,8192]{2,1,0:T(8,128)} %get-tuple-element.365, ...), kind=kLoop, calls=%fused_computation.26.clone.1.clone | loop fusion | bytes 1048608 | tf_op jit(solution)/shard_map/while/body/eval_jaxpr/slice | solution.py:45
  143.4 1.1 multiply_reduce_fusion.14
  146.3 3.1 %constant_dynamic-slice_fusion.23 = (f32[1,1,8192]{2,1,0:T(1,128)S(1)}, f32[1,1,8192]{2,1,0:T(1,128)S(1)}, f32[1,1,8192]{2,1,0:T(1,128)S(1)}, f32[1,1,8192]{2,1,...) fusion(f32[16,8,8192]{2,1,0:T(8,128)} %get-tuple-element.365, ...), kind=kLoop, calls=%fused_computation.26.clone.1.clone | loop fusion | bytes 1048608 | tf_op jit(solution)/shard_map/while/body/eval_jaxpr/slice | solution.py:45
  150.9 1.1 multiply_reduce_fusion.14
  153.1 0.7 bitcast_dynamic-update-slice_fusion.4
  153.8 2.9 %constant_dynamic-slice_fusion.23 = (f32[1,1,8192]{2,1,0:T(1,128)S(1)}, f32[1,1,8192]{2,1,0:T(1,128)S(1)}, f32[1,1,8192]{2,1,0:T(1,128)S(1)}, f32[1,1,8192]{2,1,...) fusion(f32[16,8,8192]{2,1,0:T(8,128)} %get-tuple-element.365, ...), kind=kLoop, calls=%fused_computation.26.clone.1.clone | loop fusion | bytes 1048608 | tf_op jit(solution)/shard_map/while/body/eval_jaxpr/slice | solution.py:45
  158.2 1.1 multiply_reduce_fusion.14
  160.4 0.7 bitcast_dynamic-update-slice_fusion.4
  161.1 3.3 %constant_dynamic-slice_fusion.23 = (f32[1,1,8192]{2,1,0:T(1,128)S(1)}, f32[1,1,8192]{2,1,0:T(1,128)S(1)}, f32[1,1,8192]{2,1,0:T(1,128)S(1)}, f32[1,1,8192]{2,1,...) fusion(f32[16,8,8192]{2,1,0:T(8,128)} %get-tuple-element.365, ...), kind=kLoop, calls=%fused_computation.26.clone.1.clone | loop fusion | bytes 1048608 | tf_op jit(solution)/shard_map/while/body/eval_jaxpr/slice | solution.py:45
  165.9 1.1 multiply_reduce_fusion.14
  168.8 3.1 %constant_dynamic-slice_fusion.23 = (f32[1,1,8192]{2,1,0:T(1,128)S(1)}, f32[1,1,8192]{2,1,0:T(1,128)S(1)}, f32[1,1,8192]{2,1,0:T(1,128)S(1)}, f32[1,1,8192]{2,1,...) fusion(f32[16,8,8192]{2,1,0:T(8,128)} %get-tuple-element.365, ...), kind=kLoop, calls=%fused_computation.26.clone.1.clone | loop fusion | bytes 1048608 | tf_op jit(solution)/shard_map/while/body/eval_jaxpr/slice | solution.py:45
  173.3 1.1 multiply_reduce_fusion.14
  176.2 2.9 %constant_dynamic-slice_fusion.23 = (f32[1,1,8192]{2,1,0:T(1,128)S(1)}, f32[1,1,8192]{2,1,0:T(1,128)S(1)}, f32[1,1,8192]{2,1,0:T(1,128)S(1)}, f32[1,1,8192]{2,1,...) fusion(f32[16,8,8192]{2,1,0:T(8,128)} %get-tuple-element.365, ...), kind=kLoop, calls=%fused_computation.26.clone.1.clone | loop fusion | bytes 1048608 | tf_op jit(solution)/shard_map/while/body/eval_jaxpr/slice | solution.py:45
  180.6 1.1 multiply_reduce_fusion.14
  183.5 3.0 %constant_dynamic-slice_fusion.23 = (f32[1,1,8192]{2,1,0:T(1,128)S(1)}, f32[1,1,8192]{2,1,0:T(1,128)S(1)}, f32[1,1,8192]{2,1,0:T(1,128)S(1)}, f32[1,1,8192]{2,1,...) fusion(f32[16,8,8192]{2,1,0:T(8,128)} %get-tuple-element.365, ...), kind=kLoop, calls=%fused_computation.26.clone.1.clone | loop fusion | bytes 1048608 | tf_op jit(solution)/shard_map/while/body/eval_jaxpr/slice | solution.py:45
  188.0 1.1 multiply_reduce_fusion.14
  190.9 3.0 %constant_dynamic-slice_fusion.23 = (f32[1,1,8192]{2,1,0:T(1,128)S(1)}, f32[1,1,8192]{2,1,0:T(1,128)S(1)}, f32[1,1,8192]{2,1,0:T(1,128)S(1)}, f32[1,1,8192]{2,1,...) fusion(f32[16,8,8192]{2,1,0:T(8,128)} %get-tuple-element.365, ...), kind=kLoop, calls=%fused_computation.26.clone.1.clone | loop fusion | bytes 1048608 | tf_op jit(solution)/shard_map/while/body/eval_jaxpr/slice | solution.py:45
  195.4 1.1 multiply_reduce_fusion.14
  198.3 3.0 %constant_dynamic-slice_fusion.23 = (f32[1,1,8192]{2,1,0:T(1,128)S(1)}, f32[1,1,8192]{2,1,0:T(1,128)S(1)}, f32[1,1,8192]{2,1,0:T(1,128)S(1)}, f32[1,1,8192]{2,1,...) fusion(f32[16,8,8192]{2,1,0:T(8,128)} %get-tuple-element.365, ...), kind=kLoop, calls=%fused_computation.26.clone.1.clone | loop fusion | bytes 1048608 | tf_op jit(solution)/shard_map/while/body/eval_jaxpr/slice | solution.py:45
  202.7 1.1 multiply_reduce_fusion.14
  205.6 3.0 %constant_dynamic-slice_fusion.23 = (f32[1,1,8192]{2,1,0:T(1,128)S(1)}, f32[1,1,8192]{2,1,0:T(1,128)S(1)}, f32[1,1,8192]{2,1,0:T(1,128)S(1)}, f32[1,1,8192]{2,1,...) fusion(f32[16,8,8192]{2,1,0:T(8,128)} %get-tuple-element.365, ...), kind=kLoop, calls=%fused_computation.26.clone.1.clone | loop fusion | bytes 1048608 | tf_op jit(solution)/shard_map/while/body/eval_jaxpr/slice | solution.py:45
  210.1 1.1 multiply_reduce_fusion.14
  213.0 3.1 %constant_dynamic-slice_fusion.23 = (f32[1,1,8192]{2,1,0:T(1,128)S(1)}, f32[1,1,8192]{2,1,0:T(1,128)S(1)}, f32[1,1,8192]{2,1,0:T(1,128)S(1)}, f32[1,1,8192]{2,1,...) fusion(f32[16,8,8192]{2,1,0:T(8,128)} %get-tuple-element.365, ...), kind=kLoop, calls=%fused_computation.26.clone.1.clone | loop fusion | bytes 1048608 | tf_op jit(solution)/shard_map/while/body/eval_jaxpr/slice | solution.py:45
  217.6 1.1 multiply_reduce_fusion.14
  220.5 3.0 %constant_dynamic-slice_fusion.23 = (f32[1,1,8192]{2,1,0:T(1,128)S(1)}, f32[1,1,8192]{2,1,0:T(1,128)S(1)}, f32[1,1,8192]{2,1,0:T(1,128)S(1)}, f32[1,1,8192]{2,1,...) fusion(f32[16,8,8192]{2,1,0:T(8,128)} %get-tuple-element.365, ...), kind=kLoop, calls=%fused_computation.26.clone.1.clone | loop fusion | bytes 1048608 | tf_op jit(solution)/shard_map/while/body/eval_jaxpr/slice | solution.py:45
  224.9 1.1 multiply_reduce_fusion.14
  227.8 3.0 %constant_dynamic-slice_fusion.23 = (f32[1,1,8192]{2,1,0:T(1,128)S(1)}, f32[1,1,8192]{2,1,0:T(1,128)S(1)}, f32[1,1,8192]{2,1,0:T(1,128)S(1)}, f32[1,1,8192]{2,1,...) fusion(f32[16,8,8192]{2,1,0:T(8,128)} %get-tuple-element.365, ...), kind=kLoop, calls=%fused_computation.26.clone.1.clone | loop fusion | bytes 1048608 | tf_op jit(solution)/shard_map/while/body/eval_jaxpr/slice | solution.py:45
  232.3 1.1 multiply_reduce_fusion.14
  235.1 3.1 %constant_dynamic-slice_fusion.23 = (f32[1,1,8192]{2,1,0:T(1,128)S(1)}, f32[1,1,8192]{2,1,0:T(1,128)S(1)}, f32[1,1,8192]{2,1,0:T(1,128)S(1)}, f32[1,1,8192]{2,1,...) fusion(f32[16,8,8192]{2,1,0:T(8,128)} %get-tuple-element.365, ...), kind=kLoop, calls=%fused_computation.26.clone.1.clone | loop fusion | bytes 1048608 | tf_op jit(solution)/shard_map/while/body/eval_jaxpr/slice | solution.py:45
  239.7 1.1 multiply_reduce_fusion.14
  242.6 3.2 %constant_dynamic-slice_fusion.23 = (f32[1,1,8192]{2,1,0:T(1,128)S(1)}, f32[1,1,8192]{2,1,0:T(1,128)S(1)}, f32[1,1,8192]{2,1,0:T(1,128)S(1)}, f32[1,1,8192]{2,1,...) fusion(f32[16,8,8192]{2,1,0:T(8,128)} %get-tuple-element.365, ...), kind=kLoop, calls=%fused_computation.26.clone.1.clone | loop fusion | bytes 1048608 | tf_op jit(solution)/shard_map/while/body/eval_jaxpr/slice | solution.py:45
  247.3 1.1 multiply_reduce_fusion.14
  250.2 6.9 %fusion.25 = bf16[1,1,128,8192]{3,2,1,0:T(8,128)(2,1)} fusion(bf16[128,16384]{1,0:T(8,128)(2,1)} %bitcast.259, f32[128,8192]{1,0:T(8,128)} %bitcast.235, f32[8192]{0:T(1024)S(1)} %bitcast.293, f32[16,8,8192]{2,1,0:T(8,128)} %get-tuple-element.46), kind=kLoop, calls=%fused_computation.94 | loop fusion | flops 9437184 | bytes 12615680 | tf_op jit(solution)/shard_map/broadcast_in_dim | solution.py:148
  258.2 1.1 pad_maximum_fusion.1
  260.0 0.9 fusion.28
  260.9 2.4 fusion.34
  263.9 1.0 copy.52
  (298 shorter events, 58.5 us)
Async XLA Ops:
  0.6 24.1 %copy-start.12 = (s32[1,1,8]{2,1,0:T(1,128)S(1)}, s32[1,1,8]{2,1,0:T(1,128)}, u32[]{:S(2)}) copy-start(s32[1,1,8]{2,1,0:T(1,128)} %param.30) | copy-start | bytes 100
  0.6 39.1 %copy-start.9 = (f32[1,8192]{1,0:T(1,128)S(1)}, f32[1,8192]{1,0:T(1,128)}, u32[]{:S(2)}) copy-start(f32[1,8192]{1,0:T(1,128)} %param.22) | copy-start | bytes 98308
  0.7 39.1 %copy-start.2 = (bf16[1,1,128,8192]{3,2,1,0:T(8,128)(2,1)S(1)}, bf16[1,1,128,8192]{3,2,1,0:T(8,128)(2,1)}, u32[]{:S(2)}) copy-start(bf16[1,1,128,8192]{3,2,1,0:T(8,128)(2,1)} %param.18) | copy-start | bytes 6291460
  0.7 44.4 %all-to-all-start.2 = ((bf16[2,8,3072]{2,0,1:T(2,128)(2,1)}), bf16[2,8,3072]{2,0,1:T(2,128)(2,1)S(1)}, u32[]{:S(2)}, u32[]{:S(2)}) async-start(bf16[2,8,3072]{2,0,1:T(2,128)(2,1)} %bitcast.291), calls=%async_computation.2 | async-start | bytes 196608 | tf_op jit(solution)/shard_map/all_to_all | solution.py:119
  24.0 21.0 %copy-start.11 = (bf16[1,1,128,32]{2,3,1,0:T(8,128)(2,1)S(1)}, bf16[1,1,128,32]{2,3,1,0:T(8,128)(2,1)}, u32[]{:S(2)}) copy-start(bf16[1,1,128,32]{2,3,1,0:T(8,128)(2,1)} %param.19) | copy-start | bytes 24580
  24.0 30.9 %copy-start.4 = (f32[1,2,16,8192]{3,2,1,0:T(8,128)S(1)}, f32[1,2,16,8192]{3,2,1,0:T(8,128)}, u32[]{:S(2)}) copy-start(f32[1,2,16,8192]{3,2,1,0:T(8,128)} %param.24) | copy-start | bytes 3145732
  47.5 12.0 %all-to-all-start.3 = ((bf16[8,2,1536]{2,1,0:T(2,128)(2,1)}), bf16[8,2,1536]{2,1,0:T(2,128)(2,1)S(1)}, u32[]{:S(2)}, u32[]{:S(2)}) async-start(bf16[8,2,1536]{2,1,0:T(2,128)(2,1)} %reshape.389), calls=%async_computation.3 | async-start | bytes 98304 | tf_op jit(solution)/shard_map/all_to_all | solution.py:131
  55.3 14.7 %copy-start.5 = (bf16[1,1,128,2048]{3,2,1,0:T(8,128)(2,1)S(1)}, bf16[1,1,128,2048]{3,2,1,0:T(8,128)(2,1)}, u32[]{:S(2)}) copy-start(bf16[1,1,128,2048]{3,2,1,0:T(8,128)(2,1)} %param.26) | copy-start | bytes 1572868
  57.1 14.1 %copy-start.6 = (f32[1,16,8192]{2,1,0:T(8,128)S(1)}, f32[1,16,8192]{2,1,0:T(8,128)}, u32[]{:S(2)}) copy-start(f32[1,16,8192]{2,1,0:T(8,128)} %param.20) | copy-start | bytes 1572868
  59.5 20.4 %all-to-all-start = ((f32[2,8,16384]{2,0,1:T(2,128)}), f32[2,8,16384]{2,0,1:T(2,128)S(1)}, u32[]{:S(2)}, u32[]{:S(2)}) async-start(f32[2,8,16384]{2,0,1:T(2,128)} %copy.39), calls=%async_computation | async-start | bytes 2097152 | tf_op jit(solution)/shard_map/all_to_all | solution.py:117
  66.8 20.3 %copy-start.7 = (f32[1,4,8192]{2,1,0:T(4,128)S(1)}, f32[1,4,8192]{2,1,0:T(4,128)}, u32[]{:S(2)}) copy-start(f32[1,4,8192]{2,1,0:T(4,128)} %param.21) | copy-start | bytes 393220
  79.9 7.7 %copy-start.1 = (f32[2,8,16384]{2,0,1:T(2,128)}, f32[2,8,16384]{2,0,1:T(2,128)S(1)}, u32[]{:S(2)}) copy-start(f32[2,8,16384]{2,0,1:T(2,128)S(1)} %all-to-all-done) | copy-start | bytes 3145732
  79.9 26.3 %all-to-all-start.4 = ((bf16[8,8,8192]{2,0,1:T(8,128)(2,1)}), bf16[8,8,8192]{2,0,1:T(8,128)(2,1)S(1)}, u32[]{:S(2)}, u32[]{:S(2)}) async-start(bf16[8,8,8192]{2,0,1:T(8,128)(2,1)} %copy.44), calls=%async_computation.4 | async-start | bytes 2097152 | tf_op jit(solution)/shard_map/all_to_all | solution.py:120
  106.3 18.1 %all-to-all-start.1 = ((f32[8,1,1,16384]{3,2,1,0:T(1,128)}), f32[8,1,1,16384]{3,2,1,0:T(1,128)S(1)}, u32[]{:S(2)}, u32[]{:S(2)}) async-start(f32[8,1,1,16384]{3,2,1,0:T(1,128)} %copy.40), calls=%async_computation.1 | async-start | bytes 1048576 | tf_op jit(solution)/shard_map/all_to_all | solution.py:127
  124.4 132.7 %all-to-all-start.5 = ((bf16[8,8,1,8192]{3,1,2,0:T(8,128)(2,1)}), bf16[8,8,1,8192]{3,1,2,0:T(8,128)(2,1)S(1)}, u32[]{:S(2)}, u32[]{:S(2)}) async-start(bf16[8,8,1,8192]{3,1,2,0:T(8,128)(2,1)} %bitcast.71), calls=%async_computation.5 | async-start | bytes 2097152 | tf_op jit(solution)/shard_map/all_to_all | solution.py:132
  131.7 118.5 %copy-start.10 = (f32[1,8192]{1,0:T(1,128)S(1)}, f32[1,8192]{1,0:T(1,128)}, u32[]{:S(2)}) copy-start(f32[1,8192]{1,0:T(1,128)} %param.23) | copy-start | bytes 98308
  250.2 6.9 %copy-start = (f32[16,8192]{1,0:T(8,128)}, f32[16,8192]{1,0:T(8,128)S(1)}, u32[]{:S(2)}) copy-start(f32[16,8192]{1,0:T(8,128)S(1)} %get-tuple-element.47) | copy-start | bytes 1572868
  258.2 1.7 copy-start.3
  259.6 1.2 copy-start.8
where the time goes:
time: 268 us; the launch traced here: 265 us
  local copies, waits for them, and re-layouts  98.9 us (37%)
  other arithmetic  69.9 us (26%)
  starting transfers between devices  39.7 us (15%)
  waiting for transfers between devices  25.7 us (10%)
  blocking collectives  25.3 us (9%)
    slice x16, local copies, waits for them, and re-layouts, advance_block(): signal_rows[inner]  48.6 us
    reduce_sum x48, other arithmetic, advance_block(): produced.append(jnp.sum(c_rows[inner][:, None] * ssm_state, axis=0))  38.1 us
    all_gather x1, blocking collectives, on_device(): lax.all_gather(kv_ids[0], 'pool', axis=0, tiled=True)  15 us
    all_to_all x1, waiting for transfers between devices, on_device(): lax.all_to_all(block_rows, 'pool', split_axis=1, concat_axis=0, tiled=True)  14.7 us
    dynamic_update_slice x16, local copies, waits for them, and re-layouts, mixer(): lax.scan(advance_block, start_state, (rate_blocks, signal_blocks, b_block...  11.7 us
    dynamic_slice x16, local copies, waits for them, and re-layouts, mixer(): lax.scan(advance_block, start_state, (rate_blocks, signal_blocks, b_block...  11.2 us
    all_gather x1, blocking collectives, on_device(): lax.all_gather(state_slot[0], 'pool', axis=0, tiled=True)  10.4 us
    mul x1, other arithmetic, mixer(): signal = jax.nn.silu(convolved)  8.91 us
  transfers between devices with their start and end apart: 6, of which 3 were waited for; matrix products, arithmetic and copies ran while one was open for 60% of the time, Pallas kernels for 0%

commit v1 on v0

v1 whole, which is shorter than its diff:
```python
import functools
import math

import jax
import jax.numpy as jnp
from jax import lax
from jax.experimental import pallas as pl
from jax.experimental.pallas import tpu as pltpu
from jax.sharding import PartitionSpec as P

DI = 8192
NS = 16
KW = 4
HD = 128
HQ = 16
HK = 4
NEW_TOKENS = 128
BLK = 64
KVW = 1024
LANES = 128
LIVE = 4
PIECE = DI // 8
GROUPS = PIECE // LANES
CONV_ROWS = 32
ST_ROWS = GROUPS * NS + CONV_ROWS
LOG2E = math.log2(math.e)
MESH = pl.DeviceIdType.MESH
BF = jnp.bfloat16
F32 = jnp.float32


def fetch_kernel(
    n,
    ids_ref,
    state_ref,
    conv_ref,
    kv_ref,
    st_out,
    kv_out,
    ids_all,
    ids_s,
    table,
    table_s,
    st_send,
    st_hold,
    st_send2,
    kv_send,
    kv_hold,
    kv_send2,
    local_sem,
    send_sem,
    recv_sem,
):
    me = lax.axis_index("pool")
    slots_here = state_ref.shape[0]
    blocks_here = kv_ref.shape[0]
    maxb = kv_out.shape[1]

    barrier = pltpu.get_barrier_semaphore()
    for k in range(1, n):
        pl.semaphore_signal(
            barrier, inc=1, device_id={"pool": lax.rem(me + k, n)}, device_id_type=MESH
        )
    pl.semaphore_wait(barrier, n - 1)

    def push(kind, k, src, dst):
        copy = pltpu.make_async_remote_copy(
            src_ref=src,
            dst_ref=dst,
            send_sem=send_sem.at[kind, k],
            recv_sem=recv_sem.at[kind, k],
            device_id={"pool": lax.rem(me + k, n)},
            device_id_type=MESH,
        )
        copy.start()
        return copy

    def peer(k):
        return lax.rem(me + k, n)

    copies = [push(0, k, ids_ref, ids_all.at[me]) for k in range(1, n)]
    ids_all[me] = ids_ref[...]
    for copy in copies:
        copy.wait()

    lane = lax.broadcasted_iota(jnp.int32, (8, LANES), 1)
    hit = jnp.zeros((8, LANES), jnp.int32)
    for r in range(n):
        hit = jnp.maximum(hit, (ids_all[r, :maxb] == lane).astype(jnp.int32))
    named = jnp.broadcast_to(jnp.max(hit, axis=0, keepdims=True), (8, LANES))
    rank = jnp.zeros((8, LANES), jnp.int32)
    inner = lax.rem(lane, blocks_here)
    for d in range(1, blocks_here):
        rank = rank + jnp.where(inner >= d, pltpu.roll(named, d, axis=1), 0)
    table[0:8] = named
    table[8:16] = rank
    to_s = [
        pltpu.make_async_copy(ids_all, ids_s, local_sem.at[0]),
        pltpu.make_async_copy(table, table_s, local_sem.at[1]),
    ]
    for copy in to_s:
        copy.start()
    for copy in to_s:
        copy.wait()

    slot = jnp.int32(0)
    for r in range(n):
        rel = ids_s[r, maxb, 0] - me * slots_here
        slot = jnp.where((rel >= 0) & (rel < slots_here), rel, slot)
    live = [jnp.int32(0)] * LIVE
    for j in range(blocks_here):
        is_named = table_s[0, me * blocks_here + j]
        at = table_s[8, me * blocks_here + j]
        for k in range(LIVE):
            live[k] = jnp.where((is_named == 1) & (at == k), j, live[k])

    for p in range(n):
        for j in range(GROUPS):
            lo = (p * GROUPS + j) * LANES
            st_send[p, j * NS : (j + 1) * NS, :] = state_ref[slot, :, lo : lo + LANES].astype(BF)
        st_send[p, GROUPS * NS :, :] = conv_ref[slot, p]
    st_first = [push(1, k, st_send.at[peer(k)], st_hold.at[me]) for k in range(1, n)]
    st_hold[me] = st_send[me]
    for p in range(n):
        for k in range(LIVE):
            kv_send[p, k] = kv_ref[live[k], :, p * LANES : (p + 1) * LANES]
    kv_first = [push(2, k, kv_send.at[peer(k)], kv_hold.at[me]) for k in range(1, n)]
    kv_hold[me] = kv_send[me]

    for copy in st_first:
        copy.wait()
    st_second = []
    for k in range(1, n):
        owner = ids_s[peer(k), maxb, 0] // slots_here
        st_send2[k] = st_hold[owner]
        st_second.append(push(3, k, st_send2.at[k], st_out.at[me]))
    st_out[me] = st_hold[ids_s[me, maxb, 0] // slots_here]

    for copy in kv_first:
        copy.wait()
    kv_second = []
    for k in range(1, n):
        for i in range(maxb):
            block = ids_s[peer(k), i, 0]
            kv_send2[k, i] = kv_hold[block // blocks_here, table_s[8, block]]
        kv_second.append(push(4, k, kv_send2.at[k], kv_out.at[me]))
    for i in range(maxb):
        block = ids_s[me, i, 0]
        kv_out[me, i] = kv_hold[block // blocks_here, table_s[8, block]]
    for copy in st_second + kv_second:
        copy.wait()


def fetch(state_slot, kv_ids, state_pool, conv_pool, kv_pool):
    n = lax.axis_size("pool")
    maxb = kv_ids.shape[0]
    ids = jnp.concatenate(
        [
            jnp.broadcast_to(kv_ids[:, None], (maxb, LANES)),
            jnp.broadcast_to(state_slot, (8, LANES)),
        ],
        axis=0,
    )
    slots = conv_pool.shape[0]
    conv = conv_pool.reshape(slots, KW - 1, n, GROUPS, LANES).transpose(0, 2, 3, 1, 4)
    conv = jnp.pad(conv, ((0, 0), (0, 0), (0, 0), (0, 1), (0, 0)))
    conv = conv.reshape(slots, n, CONV_ROWS, LANES)
    vmem = pl.BlockSpec(memory_space=pltpu.VMEM)
    return pl.pallas_call(
        functools.partial(fetch_kernel, n),
        out_shape=(
            jax.ShapeDtypeStruct((n, ST_ROWS, LANES), BF),
            jax.ShapeDtypeStruct((n, maxb, BLK, LANES), BF),
        ),
        in_specs=[vmem] * 4,
        out_specs=(vmem, vmem),
        scratch_shapes=[
            pltpu.VMEM((n, maxb + 8, LANES), jnp.int32),
            pltpu.SMEM((n, maxb + 8, LANES), jnp.int32),
            pltpu.VMEM((16, LANES), jnp.int32),
            pltpu.SMEM((16, LANES), jnp.int32),
            pltpu.VMEM((n, ST_ROWS, LANES), BF),
            pltpu.VMEM((n, ST_ROWS, LANES), BF),
            pltpu.VMEM((n, ST_ROWS, LANES), BF),
            pltpu.VMEM((n, LIVE, BLK, LANES), BF),
            pltpu.VMEM((n, LIVE, BLK, LANES), BF),
            pltpu.VMEM((n, maxb, BLK, LANES), BF),
            pltpu.SemaphoreType.DMA((2,)),
            pltpu.SemaphoreType.DMA((5, n)),
            pltpu.SemaphoreType.DMA((5, n)),
        ],
        compiler_params=pltpu.CompilerParams(
            collective_id=0, has_side_effects=True, vmem_limit_bytes=24 * 2**20
        ),
    )(ids, state_pool, conv, kv_pool)


CHUNKS = 2


def mixer_kernel(
    x_ref,
    g_ref,
    dt_ref,
    maps_ref,
    a_ref,
    w_ref,
    bias_ref,
    skip_ref,
    st_ref,
    out_ref,
    last_ref,
    rate_s,
    drive_s,
    y_s,
    sig_s,
    a_s,
    h_s,
    u_s,
):
    tokens = NEW_TOKENS
    for q in range(CHUNKS):
        conv_rows = st_ref[q, GROUPS * NS :, :].astype(F32)
        for j in range(GROUPS):
            col = pl.ds((q * GROUPS + j) * LANES, LANES)
            u_s[5:8, :] = conv_rows[KW * j : KW * j + KW - 1]
            u_s[8:, :] = x_ref[:, col].astype(F32)
            acc = w_ref[0:1, col] * u_s[5 : 5 + tokens, :]
            for k in range(1, KW):
                acc = acc + w_ref[k : k + 1, col] * u_s[5 + k : 5 + k + tokens, :]
            signal = acc / (1.0 + jnp.exp(-acc))
            v = dt_ref[:, col].astype(F32) + bias_ref[:, col]
            rate = jnp.maximum(v, 0.0) + jnp.log1p(jnp.exp(-jnp.abs(v)))
            sig_s[:, col] = signal
            rate_s[q, pl.ds(j, tokens, stride=8), :] = rate
            drive_s[q, pl.ds(j, tokens, stride=8), :] = rate * signal
            a_s[q, pl.ds(j, NS, stride=8), :] = -LOG2E * jnp.exp(a_ref[:, col])
            h_s[q, pl.ds(j, NS, stride=8), :] = st_ref[q, j * NS : (j + 1) * NS, :].astype(F32)

    def step(t, state):
        rows = pl.ds(pl.multiple_of(t * 8, 8), 8)
        rate = [rate_s[q, rows, :] for q in range(CHUNKS)]
        drive = [drive_s[q, rows, :] for q in range(CHUNKS)]
        total = [None] * CHUNKS
        new = []
        for m in range(NS):
            b = maps_ref[t, m]
            c = maps_ref[t, NS + m]
            for q in range(CHUNKS):
                decay = jnp.exp2(rate[q] * a_s[q, m * 8 : (m + 1) * 8, :])
                h = decay * state[m * CHUNKS + q] + drive[q] * b
                new.append(h)
                total[q] = c * h if total[q] is None else total[q] + c * h
        for q in range(CHUNKS):
            y_s[q, rows, :] = total[q]
        return tuple(new)

    first = tuple(
        h_s[q, m * 8 : (m + 1) * 8, :] for m in range(NS) for q in range(CHUNKS)
    )
    last = lax.fori_loop(0, tokens, step, first, unroll=2)
    for m in range(NS):
        for q in range(CHUNKS):
            h_s[q, m * 8 : (m + 1) * 8, :] = last[m * CHUNKS + q]
    for q in range(CHUNKS):
        for j in range(GROUPS):
            col = pl.ds((q * GROUPS + j) * LANES, LANES)
            last_ref[:, col] = h_s[q, pl.ds(j, NS, stride=8), :]
            gate = g_ref[:, col].astype(F32)
            y = y_s[q, pl.ds(j, tokens, stride=8), :] + skip_ref[:, col] * sig_s[:, col]
            out_ref[:, col] = (y * (gate / (1.0 + jnp.exp(-gate)))).astype(BF)


def mixer(x_gate, dt_raw, state_maps, a_log, conv_weight, dt_bias, d_skip, st):
    width = CHUNKS * PIECE
    steps = DI // width
    t = NEW_TOKENS
    return pl.pallas_call(
        mixer_kernel,
        grid=(steps,),
        out_shape=(
            jax.ShapeDtypeStruct((t, DI), BF),
            jax.ShapeDtypeStruct((NS, DI), F32),
        ),
        in_specs=[
            pl.BlockSpec((t, width), lambda i: (0, i)),
            pl.BlockSpec((t, width), lambda i: (0, i + steps)),
            pl.BlockSpec((t, width), lambda i: (0, i)),
            pl.BlockSpec(memory_space=pltpu.SMEM),
            pl.BlockSpec((NS, width), lambda i: (0, i)),
            pl.BlockSpec((KW, width), lambda i: (0, i)),
            pl.BlockSpec((1, width), lambda i: (0, i)),
            pl.BlockSpec((1, width), lambda i: (0, i)),
            pl.BlockSpec((CHUNKS, ST_ROWS, LANES), lambda i: (i, 0, 0)),
        ],
        out_specs=(
            pl.BlockSpec((t, width), lambda i: (0, i)),
            pl.BlockSpec((NS, width), lambda i: (0, i)),
        ),
        scratch_shapes=[
            pltpu.VMEM((CHUNKS, t * 8, LANES), F32),
            pltpu.VMEM((CHUNKS, t * 8, LANES), F32),
            pltpu.VMEM((CHUNKS, t * 8, LANES), F32),
            pltpu.VMEM((t, width), F32),
            pltpu.VMEM((CHUNKS, NS * 8, LANES), F32),
            pltpu.VMEM((CHUNKS, NS * 8, LANES), F32),
            pltpu.VMEM((t + 8, LANES), F32),
        ],
        compiler_params=pltpu.CompilerParams(vmem_limit_bytes=32 * 2**20),
        cost_estimate=pl.CostEstimate(
            flops=8 * t * DI * NS, bytes_accessed=10 * t * DI, transcendentals=t * DI * NS
        ),
    )(
        x_gate,
        x_gate,
        dt_raw,
        state_maps.astype(F32),
        a_log,
        conv_weight,
        dt_bias[None],
        d_skip[None],
        st,
    )


def attend_kernel(used_ref, q_ref, new_ref, k_ref, v_ref, out_ref):
    group = HQ // HK
    rows = group * NEW_TOKENS
    prefix = k_ref.shape[1] * BLK
    scale = 1.0 / math.sqrt(HD)
    used = used_ref[0]
    dims = (((1,), (1,)), ((), ()))
    for g in range(HK):
        q = jnp.concatenate(
            [q_ref[:, (g * group + i) * HD : (g * group + i + 1) * HD] for i in range(group)], axis=0
        )
        old_k = k_ref[g].reshape(prefix, HD)
        old_v = v_ref[g].reshape(prefix, HD)
        new_k = new_ref[:, g * HD : (g + 1) * HD]
        new_v = new_ref[:, (HK + g) * HD : (HK + g + 1) * HD]
        s_old = lax.dot_general(q, old_k, dims, preferred_element_type=F32) * scale
        s_new = lax.dot_general(q, new_k, dims, preferred_element_type=F32) * scale
        at = lax.broadcasted_iota(jnp.int32, (rows, prefix), 1)
        s_old = jnp.where(at < used * BLK, s_old, -1e30)
        key = lax.broadcasted_iota(jnp.int32, (rows, NEW_TOKENS), 1)
        query = lax.broadcasted_iota(jnp.int32, (rows, NEW_TOKENS), 0) % NEW_TOKENS
        s_new = jnp.where(key <= query, s_new, -1e30)
        top = jnp.maximum(
            jnp.max(s_old, axis=1, keepdims=True), jnp.max(s_new, axis=1, keepdims=True)
        )
        w_old = jnp.exp(s_old - top)
        w_new = jnp.exp(s_new - top)
        norm = 1.0 / (
            jnp.sum(w_old, axis=1, keepdims=True) + jnp.sum(w_new, axis=1, keepdims=True)
        )
        mixed = jnp.dot((w_old * norm).astype(BF), old_v, preferred_element_type=F32)
        mixed = mixed + jnp.dot((w_new * norm).astype(BF), new_v, preferred_element_type=F32)
        for i in range(group):
            out_ref[:, (g * group + i) * HD : (g * group + i + 1) * HD] = mixed[
                i * NEW_TOKENS : (i + 1) * NEW_TOKENS
            ].astype(BF)


def attend(queries, suffix_kv, heads, used):
    maxb = heads.shape[1]
    return pl.pallas_call(
        attend_kernel,
        grid=(1,),
        out_shape=jax.ShapeDtypeStruct((NEW_TOKENS, HQ * HD), BF),
        in_specs=[
            pl.BlockSpec(memory_space=pltpu.SMEM),
            pl.BlockSpec((NEW_TOKENS, HQ * HD), lambda i: (0, 0)),
            pl.BlockSpec((NEW_TOKENS, KVW), lambda i: (0, 0)),
            pl.BlockSpec((HK, maxb, BLK, HD), lambda i: (0, 0, 0, 0)),
            pl.BlockSpec((HK, maxb, BLK, HD), lambda i: (1, 0, 0, 0)),
        ],
        out_specs=pl.BlockSpec((NEW_TOKENS, HQ * HD), lambda i: (0, 0)),
        compiler_params=pltpu.CompilerParams(vmem_limit_bytes=32 * 2**20),
    )(used, queries, suffix_kv, heads, heads)


def fetch_any(state_slot, kv_ids, state_pool, conv_pool, kv_pool):
    n = lax.axis_size("pool")
    maxb = kv_ids.shape[0]
    slots = lax.all_gather(state_slot, "pool", axis=0, tiled=True)
    ids = lax.all_gather(kv_ids, "pool", axis=0, tiled=True)

    def move(pool, wanted, count):
        width = pool.size // pool.shape[0] // n
        rows = pool.reshape(pool.shape[0], n, width)
        held = lax.all_to_all(rows, "pool", split_axis=1, concat_axis=0, tiled=True)
        send = held.reshape(-1, width)[wanted].reshape(n, count, 1, width)
        return lax.all_to_all(send, "pool", split_axis=0, concat_axis=2, tiled=True)

    state = move(state_pool, slots, 1).reshape(NS, DI).astype(BF)
    conv = move(conv_pool, slots, 1).reshape(KW - 1, DI)
    blocks = move(kv_pool, ids, maxb).reshape(maxb, BLK, KVW // LANES, LANES)
    state = state.reshape(NS, 8, GROUPS, LANES).transpose(1, 2, 0, 3)
    conv = conv.reshape(KW - 1, 8, GROUPS, LANES).transpose(1, 2, 0, 3)
    conv = jnp.pad(conv, ((0, 0), (0, 0), (0, 1), (0, 0)))
    st = jnp.concatenate(
        [state.reshape(8, GROUPS * NS, LANES), conv.reshape(8, CONV_ROWS, LANES)], axis=1
    )
    return st, blocks.transpose(2, 0, 1, 3)


def on_device(
    x_gate,
    dt_raw,
    state_maps,
    a_log,
    conv_weight,
    dt_bias,
    d_skip,
    state_pool,
    conv_pool,
    queries,
    suffix_kv,
    kv_pool,
    state_slot,
    kv_ids,
    prefix_blocks,
):
    get = fetch if lax.axis_size("pool") == 8 else fetch_any
    st, heads = get(state_slot[0], kv_ids[0, 0], state_pool[0], conv_pool[0], kv_pool[0])
    mixed_out, last_state = mixer(
        x_gate[0, 0],
        dt_raw[0, 0],
        state_maps[0, 0],
        a_log[0],
        conv_weight[0],
        dt_bias[0],
        d_skip[0],
        st,
    )
    attended = attend(queries[0, 0], suffix_kv[0, 0], heads, prefix_blocks[0])
    return (mixed_out[None, None], last_state[None, None], attended[None, None])


def solution(mesh):
    placed = (
        P("section", ("groups", "pool"), None, None),
        P("section", ("groups", "pool"), None, None),
        P("section", ("groups", "pool"), None, None),
        P("section", None, None),
        P("section", None, None),
        P("section", None),
        P("section", None),
        P("section", ("groups", "pool"), None, None),
        P("section", ("groups", "pool"), None, None),
        P("section", ("groups", "pool"), None, None),
        P("section", ("groups", "pool"), None, None),
        P("section", ("groups", "pool"), None, None),
        P("section", ("groups", "pool")),
        P("section", ("groups", "pool"), None),
        P("section", ("groups", "pool")),
    )
    return jax.shard_map(
        on_device,
        mesh=mesh,
        in_specs=placed,
        out_specs=(
            P("section", ("groups", "pool"), None, None),
            P("section", ("groups", "pool"), None, None),
            P("section", ("groups", "pool"), None, None),
        ),
        check_vma=False,
    )
```

time: 268 us -> 107 us (0.40); the launches traced: 265 us -> 107 us
  Pallas kernels: 0 us -> 98 us
  local copies, waits for them, and re-layouts: 98.9 us -> 6.73 us
  other arithmetic: 69.9 us -> 0.01 us
  starting transfers between devices: 39.7 us -> 0 us
  waiting for transfers between devices: 25.7 us -> 0 us
  blocking collectives: 25.3 us -> 0 us
    pallas_call x0 -> x3, Pallas kernels: none -> 98 us  [the longest x1 58.2 us: fetch(): pl.pallas_call(functools.partial(fetch_kernel, n), out_shape=(jax.ShapeDt...]
    slice x19 -> x0, local copies, waits for them, and re-layouts: 49.3 us -> none  [the longest x16 48.6 us: advance_block(): signal_rows[inner]]
    all_to_all x6 -> x0, starting transfers between devices: 39.7 us -> none  [the longest x1 7.43 us: on_device(): lax.all_to_all(send_conv, 'pool', split_axis=0, concat_axis=2, tiled=True)]
    reduce_sum x48 -> x0, other arithmetic: 38.1 us -> none  [advance_block(): produced.append(jnp.sum(c_rows[inner][:, None] * ssm_state, axis=0))]
    all_to_all x6 -> x0, waiting for transfers between devices: 25.7 us -> none  [the longest x1 14.7 us: on_device(): lax.all_to_all(block_rows, 'pool', split_axis=1, concat_axis=0, tiled=True)]
    all_gather x2 -> x0, blocking collectives: 25.3 us -> none  [the longest x1 15 us: on_device(): lax.all_gather(kv_ids[0], 'pool', axis=0, tiled=True)]
    another operation x22 -> x2, local copies, waits for them, and re-layouts: 13.1 us -> 1.07 us  [fetch(): conv_pool.reshape(slots, KW - 1, n, GROUPS, LANES).transpose(0, 2, 3, 1, 4)]
    dynamic_update_slice x16 -> x0, local copies, waits for them, and re-layouts: 11.7 us -> none  [mixer(): lax.scan(advance_block, start_state, (rate_blocks, signal_blocks, b_block...]
  transfers between devices with their start and end apart: 6 -> 0, of which waited for: 3 -> 0; matrix products, arithmetic and copies ran while one was open for 60% -> 0% of each run, Pallas kernels for 0% -> 0%
where the time goes in v1:
time: 107 us
  Pallas kernels  98 us (92%)
  local copies, waits for them, and re-layouts  6.73 us (6%)
  between operations  2.12 us (2%)
    pallas_call x1, Pallas kernels, fetch(): pl.pallas_call(functools.partial(fetch_kernel, n), out_shape=(jax.ShapeDt...  58.2 us
    pallas_call x1, Pallas kernels, mixer(): pl.pallas_call(mixer_kernel, grid=(steps,), out_shape=(jax.ShapeDtypeStru...  35.9 us
    unnamed x21, local copies, waits for them, and re-layouts  4.88 us
    pallas_call x1, Pallas kernels, attend(): pl.pallas_call(attend_kernel, grid=(1,), out_shape=jax.ShapeDtypeStruct((...  3.97 us

profile of v1, /device:TPU:14, one launch (start us, length us, event | category | flops | bytes accessed | tf_op | source)
XLA Modules:
  0.0 106.9 jit_solution(12434328012997574024)
XLA Ops:
  0.6 0.0 copy-start.3
  0.6 0.0 copy-start.2
  2.0 0.7 concatenate.5
  2.7 0.1 concatenate.6.ids_ref
  2.7 0.8 copy.18
  3.6 1.0 reshape_squeeze.3
  4.6 0.1 copy.21
  4.6 0.1 pad.5
  4.7 0.0 copy-start
  4.7 1.2 %copy-done = f32[1,2,16,8192]{3,2,1,0:T(8,128)S(1)} copy-done((f32[1,2,16,8192]{3,2,1,0:T(8,128)S(1)}, f32[1,2,16,8192]{3,2,1,0:T(8,128)}, u32[]{:S(2)}) %copy-start) | copy-done | bytes 1048600
  5.9 0.0 copy-start.1
  5.9 1.2 %copy-done.1 = bf16[1,8,64,1024]{3,2,1,0:T(8,128)(2,1)S(1)} copy-done((bf16[1,8,64,1024]{3,2,1,0:T(8,128)(2,1)S(1)}, bf16[1,8,64,1024]{3,2,1,0:T(8,128)(2,1)}, u32[]{:S(2)}) %copy-start.1) | copy-done | bytes 1048600
  7.2 0.0 copy-start.4
  7.2 58.2 %shard_map.166 = (bf16[8,160,128]{2,1,0:T(8,128)(2,1)S(1)}, bf16[8,8,64,128]{3,2,1,0:T(8,128)(2,1)S(1)}) custom-call(s32[16,128]{1,0:T(8,128)S(1)} %concatenate.6.ids_ref, f32[2,16,8192]{2,1,0:T(8,128)S(1)} %bitcast.25, bf16[2,8,32,128]{3,2,1,0:T(8,128)(2,1)S(1)} %bitcast.27, bf16[8,64,1024]{2,1,0:T(8,128)(2,1)S(1)} %bitcast.26), custom_call_target="tpu_custom_call" | custom-call | tf_op jit(solution)/shard_map/pallas_call | solution.py:169
  65.3 0.0 copy-start.6
  65.4 0.0 copy-start.7
  65.4 0.0 copy-start.8
  65.4 0.0 copy-start.9
  65.4 0.0 copy-done.3
  65.4 0.0 copy-done.2
  65.4 4.0 %shard_map.168 = bf16[128,2048]{1,0:T(8,128)(2,1)} custom-call(s32[1]{0:T(128)} %bitcast.24.used_ref, bf16[128,2048]{1,0:T(8,128)(2,1)S(1)} %bitcast.28, bf16[128,1024]{1,0:T(8,128)(2,1)S(1)} %bitcast.29, bf16[8,8,64,128]{3,2,1,0:T(8,128)(2,1)S(1)} %get-tuple-element.10.k_ref.v_ref, bf16[8,8,64,128]{3,2,1,0:T(8,128)(2,1)S(1)} %get-tuple-element.10.k_ref.v_ref), custom_call_target="tpu_custom_call" | custom-call | tf_op jit(solution)/shard_map/pallas_call | solution.py:366
  69.4 0.0 copy-done.4
  69.4 0.0 copy-done.6
  69.4 0.0 copy-done.7
  69.4 0.0 copy-done.8
  69.4 0.0 copy-done.9
  69.4 0.0 copy-start.5
  69.4 1.6 %copy-done.5 = bf16[1,1,128,8192]{3,2,1,0:T(8,128)(2,1)S(1)} copy-done((bf16[1,1,128,8192]{3,2,1,0:T(8,128)(2,1)S(1)}, bf16[1,1,128,8192]{3,2,1,0:T(8,128)(2,1)}, u32[]{:S(2)}) %copy-start.5) | copy-done | bytes 2097176
  71.0 35.9 %shard_map.167 = (bf16[128,8192]{1,0:T(8,128)(2,1)}, f32[16,8192]{1,0:T(8,128)}) custom-call(bf16[128,16384]{1,0:T(8,128)(2,1)S(1)} %bitcast.30, bf16[128,16384]{1,0:T(8,128)(2,1)S(1)} %bitcast.31, bf16[128,8192]{1,0:T(8,128)(2,1)S(1)} %bitcast.32, f32[128,32]{1,0:T(8,128)S(1)} %bitcast_convert_fusion.maps_ref, f32[16,8192]{1,0:T(8,128)S(1)} %bitcast.33, ...), custom_call_target="tpu_custom_call" | custom-call | flops 134217728 | bytes 10485760 | tf_op jit(solution)/shard_map/pallas_call | solution.py:278
  (1 shorter events, 0.0 us)
Async XLA Ops:
  0.6 64.8 %copy-start.3 = (bf16[1,1,128,1024]{3,2,1,0:T(8,128)(2,1)S(1)}, bf16[1,1,128,1024]{3,2,1,0:T(8,128)(2,1)}, u32[]{:S(2)}) copy-start(bf16[1,1,128,1024]{3,2,1,0:T(8,128)(2,1)} %param.25) | copy-start | bytes 786436
  0.6 64.8 %copy-start.2 = (bf16[1,1,128,2048]{3,2,1,0:T(8,128)(2,1)S(1)}, bf16[1,1,128,2048]{3,2,1,0:T(8,128)(2,1)}, u32[]{:S(2)}) copy-start(bf16[1,1,128,2048]{3,2,1,0:T(8,128)(2,1)} %param.24) | copy-start | bytes 1572868
  4.7 1.2 %copy-start = (f32[1,2,16,8192]{3,2,1,0:T(8,128)S(1)}, f32[1,2,16,8192]{3,2,1,0:T(8,128)}, u32[]{:S(2)}) copy-start(f32[1,2,16,8192]{3,2,1,0:T(8,128)} %param.22) | copy-start | bytes 3145732
  5.9 1.2 %copy-start.1 = (bf16[1,8,64,1024]{3,2,1,0:T(8,128)(2,1)S(1)}, bf16[1,8,64,1024]{3,2,1,0:T(8,128)(2,1)}, u32[]{:S(2)}) copy-start(bf16[1,8,64,1024]{3,2,1,0:T(8,128)(2,1)} %param.26) | copy-start | bytes 3145732
  7.2 62.2 %copy-start.4 = (bf16[1,1,128,16384]{3,2,1,0:T(8,128)(2,1)S(1)}, bf16[1,1,128,16384]{3,2,1,0:T(8,128)(2,1)}, u32[]{:S(2)}) copy-start(bf16[1,1,128,16384]{3,2,1,0:T(8,128)(2,1)} %param.15) | copy-start | bytes 12582916
  65.3 4.0 %copy-start.6 = (f32[1,16,8192]{2,1,0:T(8,128)S(1)}, f32[1,16,8192]{2,1,0:T(8,128)}, u32[]{:S(2)}) copy-start(f32[1,16,8192]{2,1,0:T(8,128)} %param.18) | copy-start | bytes 1572868
  65.4 4.0 %copy-start.7 = (f32[1,4,8192]{2,1,0:T(4,128)S(1)}, f32[1,4,8192]{2,1,0:T(4,128)}, u32[]{:S(2)}) copy-start(f32[1,4,8192]{2,1,0:T(4,128)} %param.19) | copy-start | bytes 393220
  65.4 4.0 %copy-start.8 = (f32[1,8192]{1,0:T(1,128)S(1)}, f32[1,8192]{1,0:T(1,128)}, u32[]{:S(2)}) copy-start(f32[1,8192]{1,0:T(1,128)} %bias_ref.1) | copy-start | bytes 98308
  65.4 4.0 %copy-start.9 = (f32[1,8192]{1,0:T(1,128)S(1)}, f32[1,8192]{1,0:T(1,128)}, u32[]{:S(2)}) copy-start(f32[1,8192]{1,0:T(1,128)} %skip_ref.1) | copy-start | bytes 98308
  69.4 1.6 %copy-start.5 = (bf16[1,1,128,8192]{3,2,1,0:T(8,128)(2,1)S(1)}, bf16[1,1,128,8192]{3,2,1,0:T(8,128)(2,1)}, u32[]{:S(2)}) copy-start(bf16[1,1,128,8192]{3,2,1,0:T(8,128)(2,1)} %param.16) | copy-start | bytes 6291460

commit v2 on v1

--- a/solution.py
+++ b/solution.py
@@ -29,14 +29,90 @@
 F32 = jnp.float32
 
 
-def fetch_kernel(
+CHUNKS = 2
+
+
+def mix(i, maps_ref, a_ref, w_ref, skip_ref, x_ref, st_ref, out_ref, last_ref,
+        rate_s, gate_s, drive_s, y_s, sig_s, a_s, h_s, u_s):
+    tokens = NEW_TOKENS
+    width = CHUNKS * PIECE
+
+    def columns(q, j):
+        return pl.ds(pl.multiple_of(i * width + (q * GROUPS + j) * LANES, LANES), LANES)
+
+    for q in range(CHUNKS):
+        p = i * CHUNKS + q
+        conv_rows = st_ref[p, GROUPS * NS :, :].astype(F32)
+        for j in range(GROUPS):
+            col = columns(q, j)
+            here = (q * GROUPS + j) * LANES
+            u_s[5:8, :] = conv_rows[KW * j : KW * j + KW - 1]
+            u_s[8:, :] = x_ref[:, col].astype(F32)
+            acc = w_ref[0:1, col] * u_s[5 : 5 + tokens, :]
+            for k in range(1, KW):
+                acc = acc + w_ref[k : k + 1, col] * u_s[5 + k : 5 + k + tokens, :]
+            signal = acc / (1.0 + jnp.exp(-acc))
+            sig_s[:, here : here + LANES] = signal
+            rate = rate_s[p, pl.ds(j, tokens, stride=8), :]
+            drive_s[q, pl.ds(j, tokens, stride=8), :] = rate * signal
+            a_s[pl.ds(q * 8 + j, NS, stride=8 * CHUNKS), :] = -LOG2E * jnp.exp(a_ref[:, col])
+            h_s[pl.ds(q * 8 + j, NS, stride=8 * CHUNKS), :] = st_ref[
+                p, j * NS : (j + 1) * NS, :
+            ].astype(F32)
+
+    tall = 8 * CHUNKS
+
+    def step(t, state):
+        rows = pl.ds(pl.multiple_of(t * 8, 8), 8)
+        rate = jnp.concatenate([rate_s[i * CHUNKS + q, rows, :] for q in range(CHUNKS)], axis=0)
+        drive = jnp.concatenate([drive_s[q, rows, :] for q in range(CHUNKS)], axis=0)
+        total = None
+        new = []
+        for m in range(NS):
+            b = maps_ref[t, m]
+            c = maps_ref[t, NS + m]
+            decay = jnp.exp2(rate * a_s[m * tall : (m + 1) * tall, :])
+            h = decay * state[m] + drive * b
+            new.append(h)
+            total = c * h if total is None else total + c * h
+        for q in range(CHUNKS):
+            y_s[q, rows, :] = total[q * 8 : (q + 1) * 8]
+        return tuple(new)
+
+    first = tuple(h_s[m * tall : (m + 1) * tall, :] for m in range(NS))
+    last = lax.fori_loop(0, tokens, step, first, unroll=2)
+    for m in range(NS):
+        h_s[m * tall : (m + 1) * tall, :] = last[m]
+    for q in range(CHUNKS):
+        for j in range(GROUPS):
+            col = columns(q, j)
+            here = (q * GROUPS + j) * LANES
+            last_ref[:, col] = h_s[pl.ds(q * 8 + j, NS, stride=tall), :]
+            y = y_s[q, pl.ds(j, tokens, stride=8), :] + skip_ref[:, col] * sig_s[:, here : here + LANES]
+            out_ref[:, col] = (y * gate_s[:, col]).astype(BF)
+
+
+def serve_kernel(
     n,
     ids_ref,
+    maps_ref,
+    conv_ref,
+    a_ref,
+    w_ref,
+    bias_ref,
+    skip_ref,
+    state_hbm,
+    kv_hbm,
+    x_hbm,
+    dt_hbm,
+    out_ref,
+    last_ref,
+    kv_out,
     state_ref,
-    conv_ref,
     kv_ref,
+    x_ref,
+    dt_ref,
     st_out,
-    kv_out,
     ids_all,
     ids_s,
     table,
@@ -47,6 +123,14 @@
     kv_send,
     kv_hold,
     kv_send2,
+    rate_s,
+    gate_s,
+    drive_s,
+    y_s,
+    sig_s,
+    a_s,
+    h_s,
+    u_s,
     local_sem,
     send_sem,
     recv_sem,
@@ -55,6 +139,15 @@
     slots_here = state_ref.shape[0]
     blocks_here = kv_ref.shape[0]
     maxb = kv_out.shape[1]
+
+    load_state, load_kv, load_dt, load_x = [
+        pltpu.make_async_copy(src, dst, local_sem.at[2 + i])
+        for i, (src, dst) in enumerate(
+            ((state_hbm, state_ref), (kv_hbm, kv_ref), (dt_hbm, dt_ref), (x_hbm, x_ref))
+        )
+    ]
+    for copy in (load_state, load_kv, load_dt, load_x):
+        copy.start()
 
     barrier = pltpu.get_barrier_semaphore()
     for k in range(1, n):
@@ -114,6 +207,7 @@
         for k in range(LIVE):
             live[k] = jnp.where((is_named == 1) & (at == k), j, live[k])
 
+    load_state.wait()
     for p in range(n):
         for j in range(GROUPS):
             lo = (p * GROUPS + j) * LANES
@@ -121,11 +215,24 @@
         st_send[p, GROUPS * NS :, :] = conv_ref[slot, p]
     st_first = [push(1, k, st_send.at[peer(k)], st_hold.at[me]) for k in range(1, n)]
     st_hold[me] = st_send[me]
+    load_kv.wait()
     for p in range(n):
         for k in range(LIVE):
             kv_send[p, k] = kv_ref[live[k], :, p * LANES : (p + 1) * LANES]
     kv_first = [push(2, k, kv_send.at[peer(k)], kv_hold.at[me]) for k in range(1, n)]
     kv_hold[me] = kv_send[me]
+
+    load_dt.wait()
+
+    def rates(p, carry):
+        for j in range(GROUPS):
+            col = pl.ds(pl.multiple_of(p * PIECE + j * LANES, LANES), LANES)
+            v = dt_ref[:, col].astype(F32) + bias_ref[:, col]
+            rate = jnp.maximum(v, 0.0) + jnp.log1p(jnp.exp(-jnp.abs(v)))
+            rate_s[p, pl.ds(j, NEW_TOKENS, stride=8), :] = rate
+        return carry
+
+    lax.fori_loop(0, DI // PIECE, rates, 0)
 
     for copy in st_first:
         copy.wait()
@@ -136,6 +243,26 @@
         st_second.append(push(3, k, st_send2.at[k], st_out.at[me]))
     st_out[me] = st_hold[ids_s[me, maxb, 0] // slots_here]
 
+    load_x.wait()
+
+    def gates(p, carry):
+        for j in range(GROUPS):
+            col = pl.ds(pl.multiple_of(p * PIECE + j * LANES, LANES), LANES)
+            far = pl.ds(pl.multiple_of(DI + p * PIECE + j * LANES, LANES), LANES)
+            gate = x_ref[:, far].astype(F32)
+            gate_s[:, col] = gate / (1.0 + jnp.exp(-gate))
+        return carry
+
+    lax.fori_loop(0, DI // PIECE, gates, 0)
+    for copy in st_second:
+        copy.wait()
+
+    def run(i, carry):
+        mix(i, maps_ref, a_ref, w_ref, skip_ref, x_ref, st_out, out_ref, last_ref,
+            rate_s, gate_s, drive_s, y_s, sig_s, a_s, h_s, u_s)
+        return carry
+
+    run(0, 0)
     for copy in kv_first:
         copy.wait()
     kv_second = []
@@ -147,11 +274,14 @@
     for i in range(maxb):
         block = ids_s[me, i, 0]
         kv_out[me, i] = kv_hold[block // blocks_here, table_s[8, block]]
-    for copy in st_second + kv_second:
+    lax.fori_loop(1, DI // (CHUNKS * PIECE), run, 0)
+    for copy in kv_second:
         copy.wait()
 
 
-def fetch(state_slot, kv_ids, state_pool, conv_pool, kv_pool):
+def serve(
+    state_slot, kv_ids, state_pool, conv_pool, kv_pool, x_gate, dt_raw, state_maps, a_log, conv_weight, dt_bias, d_skip
+):
     n = lax.axis_size("pool")
     maxb = kv_ids.shape[0]
     ids = jnp.concatenate(
@@ -167,14 +297,22 @@
     conv = conv.reshape(slots, n, CONV_ROWS, LANES)
     vmem = pl.BlockSpec(memory_space=pltpu.VMEM)
     return pl.pallas_call(
-        functools.partial(fetch_kernel, n),
+        functools.partial(serve_kernel, n),
         out_shape=(
-            jax.ShapeDtypeStruct((n, ST_ROWS, LANES), BF),
+            jax.ShapeDtypeStruct((NEW_TOKENS, DI), BF),
+            jax.ShapeDtypeStruct((NS, DI), F32),
             jax.ShapeDtypeStruct((n, maxb, BLK, LANES), BF),
         ),
-        in_specs=[vmem] * 4,
-        out_specs=(vmem, vmem),
+        in_specs=[vmem, pl.BlockSpec(memory_space=pltpu.SMEM)]
+        + [vmem] * 5
+        + [pl.BlockSpec(memory_space=pl.ANY)] * 4,
+        out_specs=(vmem, vmem, vmem),
         scratch_shapes=[
+            pltpu.VMEM(state_pool.shape, F32),
+            pltpu.VMEM(kv_pool.shape, BF),
+            pltpu.VMEM(x_gate.shape, BF),
+            pltpu.VMEM(dt_raw.shape, BF),
+            pltpu.VMEM((n, ST_ROWS, LANES), BF),
             pltpu.VMEM((n, maxb + 8, LANES), jnp.int32),
             pltpu.SMEM((n, maxb + 8, LANES), jnp.int32),
             pltpu.VMEM((16, LANES), jnp.int32),
@@ -185,17 +323,34 @@
             pltpu.VMEM((n, LIVE, BLK, LANES), BF),
             pltpu.VMEM((n, LIVE, BLK, LANES), BF),
             pltpu.VMEM((n, maxb, BLK, LANES), BF),
-            pltpu.SemaphoreType.DMA((2,)),
+            pltpu.VMEM((DI // PIECE, NEW_TOKENS * 8, LANES), F32),
+            pltpu.VMEM((NEW_TOKENS, DI), F32),
+            pltpu.VMEM((CHUNKS, NEW_TOKENS * 8, LANES), F32),
+            pltpu.VMEM((CHUNKS, NEW_TOKENS * 8, LANES), F32),
+            pltpu.VMEM((NEW_TOKENS, CHUNKS * PIECE), F32),
+            pltpu.VMEM((CHUNKS * NS * 8, LANES), F32),
+            pltpu.VMEM((CHUNKS * NS * 8, LANES), F32),
+            pltpu.VMEM((NEW_TOKENS + 8, LANES), F32),
+            pltpu.SemaphoreType.DMA((6,)),
             pltpu.SemaphoreType.DMA((5, n)),
             pltpu.SemaphoreType.DMA((5, n)),
         ],
         compiler_params=pltpu.CompilerParams(
-            collective_id=0, has_side_effects=True, vmem_limit_bytes=24 * 2**20
+            collective_id=0, has_side_effects=True, vmem_limit_bytes=52 * 2**20
         ),
-    )(ids, state_pool, conv, kv_pool)
-
-
-CHUNKS = 2
+    )(
+        ids,
+        state_maps.astype(F32),
+        conv,
+        a_log,
+        conv_weight,
+        dt_bias[None],
+        d_skip[None],
+        state_pool,
+        kv_pool,
+        x_gate,
+        dt_raw,
+    )
 
 
 def mixer_kernel(
@@ -421,18 +576,14 @@
     kv_ids,
     prefix_blocks,
 ):
-    get = fetch if lax.axis_size("pool") == 8 else fetch_any
-    st, heads = get(state_slot[0], kv_ids[0, 0], state_pool[0], conv_pool[0], kv_pool[0])
-    mixed_out, last_state = mixer(
-        x_gate[0, 0],
-        dt_raw[0, 0],
-        state_maps[0, 0],
-        a_log[0],
-        conv_weight[0],
-        dt_bias[0],
-        d_skip[0],
-        st,
-    )
+    inputs = (x_gate[0, 0], dt_raw[0, 0], state_maps[0, 0])
+    params = (a_log[0], conv_weight[0], dt_bias[0], d_skip[0])
+    cache = (state_slot[0], kv_ids[0, 0], state_pool[0], conv_pool[0], kv_pool[0])
+    if lax.axis_size("pool") == DI // PIECE:
+        mixed_out, last_state, heads = serve(*cache, *inputs, *params)
+    else:
+        st, heads = fetch_any(*cache)
+        mixed_out, last_state = mixer(*inputs, *params, st)
     attended = attend(queries[0, 0], suffix_kv[0, 0], heads, prefix_blocks[0])
     return (mixed_out[None, None], last_state[None, None], attended[None, None])
 

time: 107 us -> 88.1 us (0.82)
  the two profiles are of different devices: /device:TPU:14 before, /device:TPU:0 now
where the time goes in v2:
time: 88.1 us; the launch traced here: 87.6 us
  Pallas kernels  76.2 us (86%)
  local copies, waits for them, and re-layouts  9.47 us (11%)
  between operations  1.99 us (2%)
    pallas_call x1, Pallas kernels, serve(): pl.pallas_call(functools.partial(serve_kernel, n), out_shape=(jax.ShapeDt...  72.2 us
    unnamed x19, local copies, waits for them, and re-layouts  7.61 us
    pallas_call x1, Pallas kernels, attend(): pl.pallas_call(attend_kernel, grid=(1,), out_shape=jax.ShapeDtypeStruct((...  3.99 us

profile of v2, /device:TPU:0, one launch (start us, length us, event | category | flops | bytes accessed | tf_op | source)
XLA Modules:
  0.0 87.6 jit_solution(17258133153553426951)
XLA Ops:
  0.6 1.0 %reshape_squeeze.3 = bf16[2,3,8,8,128]{4,3,2,0,1:T(8,128)(2,1)S(1)} reshape(bf16[1,2,3,8192]{3,1,2,0:T(2,128)(2,1)} %param.23) | data formatting | bytes 196608 | tf_op jit(solution)/shard_map/reshape;squeeze | solution.py:295
  1.6 0.1 copy.21
  1.7 0.1 pad.5
  1.8 0.8 copy.18
  3.2 0.7 concatenate.5
  3.9 0.1 concatenate.6.ids_ref
  4.0 0.0 copy-start.2
  4.0 1.0 %copy-done.2 = f32[1,16,8192]{2,1,0:T(8,128)S(1)} copy-done((f32[1,16,8192]{2,1,0:T(8,128)S(1)}, f32[1,16,8192]{2,1,0:T(8,128)}, u32[]{:S(2)}) %copy-start.2) | copy-done | bytes 524312
  5.0 0.0 copy-start.4
  5.0 0.9 %copy-done.4 = f32[1,4,8192]{2,1,0:T(4,128)S(1)} copy-done((f32[1,4,8192]{2,1,0:T(4,128)S(1)}, f32[1,4,8192]{2,1,0:T(4,128)}, u32[]{:S(2)}) %copy-start.4) | copy-done | bytes 131096
  5.9 0.0 copy-start.5
  5.9 0.8 copy-done.5
  6.7 0.0 copy-start.6
  6.7 0.8 copy-done.6
  7.4 0.0 copy-start.1
  7.4 0.0 copy-start.3
  7.4 72.2 %shard_map.166 = (bf16[128,8192]{1,0:T(8,128)(2,1)}, f32[16,8192]{1,0:T(8,128)S(1)}, bf16[8,8,64,128]{3,2,1,0:T(8,128)(2,1)}) custom-call(s32[16,128]{1,0:T(8,128)S(1)} %concatenate.6.ids_ref, f32[128,32]{1,0:T(8,128)S(1)} %bitcast_convert_fusion.maps_ref, bf16[2,8,32,128]{3,2,1,0:T(8,128)(2,1)S(1)} %bitcast.25, f32[16,8192]{1,0:T(8,128)S(1)} %bitcast.28, ...), custom_call_target="tpu_custom_call" | custom-call | tf_op jit(solution)/shard_map/pallas_call | solution.py:299
  80.3 0.0 copy-done.1
  80.3 0.0 copy-done.3
  80.3 0.0 copy-start
  80.3 1.2 %copy-done = bf16[8,8,64,128]{3,2,1,0:T(8,128)(2,1)S(1)} copy-done((bf16[8,8,64,128]{3,2,1,0:T(8,128)(2,1)S(1)}, bf16[8,8,64,128]{3,2,1,0:T(8,128)(2,1)}, u32[]{:S(2)}) %copy-start) | copy-done | bytes 1048600
  81.5 0.0 copy-start.7
  81.5 4.0 %shard_map.167 = bf16[128,2048]{1,0:T(8,128)(2,1)} custom-call(s32[1]{0:T(128)} %bitcast.24.used_ref, bf16[128,2048]{1,0:T(8,128)(2,1)S(1)} %bitcast.27, bf16[128,1024]{1,0:T(8,128)(2,1)S(1)} %bitcast.29, bf16[8,8,64,128]{3,2,1,0:T(8,128)(2,1)S(1)} %copy-done, bf16[8,8,64,128]{3,2,1,0:T(8,128)(2,1)S(1)} %copy-done), custom_call_target="tpu_custom_call" | custom-call | tf_op jit(solution)/shard_map/pallas_call | solution.py:521
  85.5 0.0 copy-done.7
  85.5 1.3 %copy.26 = bf16[1,1,128,8192]{3,2,1,0:T(8,128)(2,1)} copy(bf16[1,1,128,8192]{3,2,1,0:T(8,128)(2,1)S(1)} %bitcast.32) | data formatting | bytes 4194304
  86.8 0.8 copy.27
  (1 shorter events, 0.0 us)
Async XLA Ops:
  4.0 1.0 %copy-start.2 = (f32[1,16,8192]{2,1,0:T(8,128)S(1)}, f32[1,16,8192]{2,1,0:T(8,128)}, u32[]{:S(2)}) copy-start(f32[1,16,8192]{2,1,0:T(8,128)} %param.18) | copy-start | bytes 1572868
  5.0 0.9 %copy-start.4 = (f32[1,4,8192]{2,1,0:T(4,128)S(1)}, f32[1,4,8192]{2,1,0:T(4,128)}, u32[]{:S(2)}) copy-start(f32[1,4,8192]{2,1,0:T(4,128)} %param.19) | copy-start | bytes 393220
  5.9 0.8 copy-start.5
  6.7 0.8 copy-start.6
  7.4 72.8 %copy-start.1 = (bf16[1,1,128,2048]{3,2,1,0:T(8,128)(2,1)S(1)}, bf16[1,1,128,2048]{3,2,1,0:T(8,128)(2,1)}, u32[]{:S(2)}) copy-start(bf16[1,1,128,2048]{3,2,1,0:T(8,128)(2,1)} %param.24) | copy-start | bytes 1572868
  7.4 72.8 %copy-start.3 = (bf16[1,1,128,1024]{3,2,1,0:T(8,128)(2,1)S(1)}, bf16[1,1,128,1024]{3,2,1,0:T(8,128)(2,1)}, u32[]{:S(2)}) copy-start(bf16[1,1,128,1024]{3,2,1,0:T(8,128)(2,1)} %param.25) | copy-start | bytes 786436
  80.3 1.2 %copy-start = (bf16[8,8,64,128]{3,2,1,0:T(8,128)(2,1)S(1)}, bf16[8,8,64,128]{3,2,1,0:T(8,128)(2,1)}, u32[]{:S(2)}) copy-start(bf16[8,8,64,128]{3,2,1,0:T(8,128)(2,1)} %get-tuple-element.8.k_ref.v_ref) | copy-start | bytes 3145732
  81.5 4.0 %copy-start.7 = (bf16[128,8192]{1,0:T(8,128)(2,1)S(1)}, bf16[128,8192]{1,0:T(8,128)(2,1)}, u32[]{:S(2)}) copy-start(bf16[128,8192]{1,0:T(8,128)(2,1)} %get-tuple-element.6) | copy-start | bytes 6291460

commit v3 on v2

--- a/solution.py
+++ b/solution.py
@@ -97,21 +97,27 @@
     ids_ref,
     maps_ref,
     conv_ref,
-    a_ref,
-    w_ref,
-    bias_ref,
-    skip_ref,
     state_hbm,
     kv_hbm,
+    dt_hbm,
+    bias_hbm,
     x_hbm,
-    dt_hbm,
-    out_ref,
-    last_ref,
+    w_hbm,
+    a_hbm,
+    skip_hbm,
+    out_hbm,
+    last_hbm,
     kv_out,
     state_ref,
     kv_ref,
+    dt_ref,
+    bias_ref,
     x_ref,
-    dt_ref,
+    w_ref,
+    a_ref,
+    skip_ref,
+    out_ref,
+    last_ref,
     st_out,
     ids_all,
     ids_s,
@@ -131,6 +137,7 @@
     a_s,
     h_s,
     u_s,
+    store_sem,
     local_sem,
     send_sem,
     recv_sem,
@@ -140,13 +147,22 @@
     blocks_here = kv_ref.shape[0]
     maxb = kv_out.shape[1]
 
-    load_state, load_kv, load_dt, load_x = [
+    loads = [
         pltpu.make_async_copy(src, dst, local_sem.at[2 + i])
         for i, (src, dst) in enumerate(
-            ((state_hbm, state_ref), (kv_hbm, kv_ref), (dt_hbm, dt_ref), (x_hbm, x_ref))
+            (
+                (state_hbm, state_ref),
+                (kv_hbm, kv_ref),
+                (dt_hbm, dt_ref),
+                (bias_hbm, bias_ref),
+                (x_hbm, x_ref),
+                (w_hbm, w_ref),
+                (a_hbm, a_ref),
+                (skip_hbm, skip_ref),
+            )
         )
     ]
-    for copy in (load_state, load_kv, load_dt, load_x):
+    for copy in loads:
         copy.start()
 
     barrier = pltpu.get_barrier_semaphore()
@@ -207,7 +223,7 @@
         for k in range(LIVE):
             live[k] = jnp.where((is_named == 1) & (at == k), j, live[k])
 
-    load_state.wait()
+    loads[0].wait()
     for p in range(n):
         for j in range(GROUPS):
             lo = (p * GROUPS + j) * LANES
@@ -215,14 +231,9 @@
         st_send[p, GROUPS * NS :, :] = conv_ref[slot, p]
     st_first = [push(1, k, st_send.at[peer(k)], st_hold.at[me]) for k in range(1, n)]
     st_hold[me] = st_send[me]
-    load_kv.wait()
-    for p in range(n):
-        for k in range(LIVE):
-            kv_send[p, k] = kv_ref[live[k], :, p * LANES : (p + 1) * LANES]
-    kv_first = [push(2, k, kv_send.at[peer(k)], kv_hold.at[me]) for k in range(1, n)]
-    kv_hold[me] = kv_send[me]
-
-    load_dt.wait()
+
+    loads[2].wait()
+    loads[3].wait()
 
     def rates(p, carry):
         for j in range(GROUPS):
@@ -243,7 +254,15 @@
         st_second.append(push(3, k, st_send2.at[k], st_out.at[me]))
     st_out[me] = st_hold[ids_s[me, maxb, 0] // slots_here]
 
-    load_x.wait()
+    loads[1].wait()
+    for p in range(n):
+        for k in range(LIVE):
+            kv_send[p, k] = kv_ref[live[k], :, p * LANES : (p + 1) * LANES]
+    kv_first = [push(2, k, kv_send.at[peer(k)], kv_hold.at[me]) for k in range(1, n)]
+    kv_hold[me] = kv_send[me]
+
+    for copy in loads[4:]:
+        copy.wait()
 
     def gates(p, carry):
         for j in range(GROUPS):
@@ -257,9 +276,19 @@
     for copy in st_second:
         copy.wait()
 
+    def stores(i):
+        width = CHUNKS * PIECE
+        col = pl.ds(i * width if isinstance(i, int) else pl.multiple_of(i * width, width), width)
+        return (
+            pltpu.make_async_copy(out_ref.at[:, col], out_hbm.at[:, col], store_sem.at[0, i]),
+            pltpu.make_async_copy(last_ref.at[:, col], last_hbm.at[:, col], store_sem.at[1, i]),
+        )
+
     def run(i, carry):
         mix(i, maps_ref, a_ref, w_ref, skip_ref, x_ref, st_out, out_ref, last_ref,
             rate_s, gate_s, drive_s, y_s, sig_s, a_s, h_s, u_s)
+        for copy in stores(i):
+            copy.start()
         return carry
 
     run(0, 0)
@@ -277,6 +306,9 @@
     lax.fori_loop(1, DI // (CHUNKS * PIECE), run, 0)
     for copy in kv_second:
         copy.wait()
+    for i in range(DI // (CHUNKS * PIECE)):
+        for copy in stores(i):
+            copy.wait()
 
 
 def serve(
@@ -296,6 +328,7 @@
     conv = jnp.pad(conv, ((0, 0), (0, 0), (0, 0), (0, 1), (0, 0)))
     conv = conv.reshape(slots, n, CONV_ROWS, LANES)
     vmem = pl.BlockSpec(memory_space=pltpu.VMEM)
+    hbm = pl.BlockSpec(memory_space=pl.ANY)
     return pl.pallas_call(
         functools.partial(serve_kernel, n),
         out_shape=(
@@ -304,14 +337,20 @@
             jax.ShapeDtypeStruct((n, maxb, BLK, LANES), BF),
         ),
         in_specs=[vmem, pl.BlockSpec(memory_space=pltpu.SMEM)]
-        + [vmem] * 5
-        + [pl.BlockSpec(memory_space=pl.ANY)] * 4,
-        out_specs=(vmem, vmem, vmem),
+        + [vmem]
+        + [hbm] * 8,
+        out_specs=(hbm, hbm, vmem),
         scratch_shapes=[
             pltpu.VMEM(state_pool.shape, F32),
             pltpu.VMEM(kv_pool.shape, BF),
+            pltpu.VMEM(dt_raw.shape, BF),
+            pltpu.VMEM((1, DI), F32),
             pltpu.VMEM(x_gate.shape, BF),
-            pltpu.VMEM(dt_raw.shape, BF),
+            pltpu.VMEM(conv_weight.shape, F32),
+            pltpu.VMEM(a_log.shape, F32),
+            pltpu.VMEM((1, DI), F32),
+            pltpu.VMEM((NEW_TOKENS, DI), BF),
+            pltpu.VMEM((NS, DI), F32),
             pltpu.VMEM((n, ST_ROWS, LANES), BF),
             pltpu.VMEM((n, maxb + 8, LANES), jnp.int32),
             pltpu.SMEM((n, maxb + 8, LANES), jnp.int32),
@@ -331,7 +370,8 @@
             pltpu.VMEM((CHUNKS * NS * 8, LANES), F32),
             pltpu.VMEM((CHUNKS * NS * 8, LANES), F32),
             pltpu.VMEM((NEW_TOKENS + 8, LANES), F32),
-            pltpu.SemaphoreType.DMA((6,)),
+            pltpu.SemaphoreType.DMA((2, DI // (CHUNKS * PIECE))),
+            pltpu.SemaphoreType.DMA((10,)),
             pltpu.SemaphoreType.DMA((5, n)),
             pltpu.SemaphoreType.DMA((5, n)),
         ],
@@ -342,14 +382,14 @@
         ids,
         state_maps.astype(F32),
         conv,
-        a_log,
-        conv_weight,
-        dt_bias[None],
-        d_skip[None],
         state_pool,
         kv_pool,
+        dt_raw,
+        dt_bias[None],
         x_gate,
-        dt_raw,
+        conv_weight,
+        a_log,
+        d_skip[None],
     )
 
 

time: 88.1 us -> 85.5 us (0.970)
  the two profiles are of different devices: /device:TPU:0 before, /device:TPU:14 now
where the time goes in v3:
time: 85.5 us; the launch traced here: 85 us
  Pallas kernels  73.5 us (86%)
  local copies, waits for them, and re-layouts  9.47 us (11%)
  between operations  1.99 us (2%)
    pallas_call x1, Pallas kernels, serve(): pl.pallas_call(functools.partial(serve_kernel, n), out_shape=(jax.ShapeDt...  69.6 us
    unnamed x19, local copies, waits for them, and re-layouts  7.61 us
    pallas_call x1, Pallas kernels, attend(): pl.pallas_call(attend_kernel, grid=(1,), out_shape=jax.ShapeDtypeStruct((...  3.99 us

profile of v3, /device:TPU:14, one launch (start us, length us, event | category | flops | bytes accessed | tf_op | source)
XLA Modules:
  0.0 85.0 jit_solution(11330880149003669271)
XLA Ops:
  0.6 1.0 %reshape_squeeze.3 = bf16[2,3,8,8,128]{4,3,2,0,1:T(8,128)(2,1)S(1)} reshape(bf16[1,2,3,8192]{3,1,2,0:T(2,128)(2,1)} %param.23) | data formatting | bytes 196608 | tf_op jit(solution)/shard_map/reshape;squeeze | solution.py:327
  1.6 0.1 copy.21
  1.7 0.1 pad.5
  1.8 0.8 copy.18
  3.2 0.7 concatenate.5
  3.9 0.1 concatenate.6.ids_ref
  4.0 0.0 copy-start.2
  4.0 1.0 %copy-done.2 = f32[1,16,8192]{2,1,0:T(8,128)S(1)} copy-done((f32[1,16,8192]{2,1,0:T(8,128)S(1)}, f32[1,16,8192]{2,1,0:T(8,128)}, u32[]{:S(2)}) %copy-start.2) | copy-done | bytes 524312
  5.0 0.0 copy-start.4
  5.0 0.9 %copy-done.4 = f32[1,4,8192]{2,1,0:T(4,128)S(1)} copy-done((f32[1,4,8192]{2,1,0:T(4,128)S(1)}, f32[1,4,8192]{2,1,0:T(4,128)}, u32[]{:S(2)}) %copy-start.4) | copy-done | bytes 131096
  5.9 0.0 copy-start.5
  5.9 0.8 copy-done.5
  6.7 0.0 copy-start.6
  6.7 0.8 copy-done.6
  7.4 0.0 copy-start.1
  7.4 0.0 copy-start.3
  7.4 69.6 %shard_map.166 = (bf16[128,8192]{1,0:T(8,128)(2,1)}, f32[16,8192]{1,0:T(8,128)S(1)}, bf16[8,8,64,128]{3,2,1,0:T(8,128)(2,1)}) custom-call(s32[16,128]{1,0:T(8,128)S(1)} %concatenate.6.ids_ref, f32[128,32]{1,0:T(8,128)S(1)} %bitcast_convert_fusion.maps_ref, bf16[2,8,32,128]{3,2,1,0:T(8,128)(2,1)S(1)} %bitcast.25, f32[2,16,8192]{2,1,0:T(8,128)} %bitcast.34, ...), custom_call_target="tpu_custom_call" | custom-call | tf_op jit(solution)/shard_map/pallas_call | solution.py:332
  77.7 0.0 copy-done.1
  77.7 0.0 copy-done.3
  77.7 0.0 copy-start
  77.7 1.2 %copy-done = bf16[8,8,64,128]{3,2,1,0:T(8,128)(2,1)S(1)} copy-done((bf16[8,8,64,128]{3,2,1,0:T(8,128)(2,1)S(1)}, bf16[8,8,64,128]{3,2,1,0:T(8,128)(2,1)}, u32[]{:S(2)}) %copy-start) | copy-done | bytes 1048600
  78.9 0.0 copy-start.7
  78.9 4.0 %shard_map.167 = bf16[128,2048]{1,0:T(8,128)(2,1)} custom-call(s32[1]{0:T(128)} %bitcast.24.used_ref, bf16[128,2048]{1,0:T(8,128)(2,1)S(1)} %bitcast.27, bf16[128,1024]{1,0:T(8,128)(2,1)S(1)} %bitcast.29, bf16[8,8,64,128]{3,2,1,0:T(8,128)(2,1)S(1)} %copy-done, bf16[8,8,64,128]{3,2,1,0:T(8,128)(2,1)S(1)} %copy-done), custom_call_target="tpu_custom_call" | custom-call | tf_op jit(solution)/shard_map/pallas_call | solution.py:561
  82.9 0.0 copy-done.7
  82.9 1.3 %copy.26 = bf16[1,1,128,8192]{3,2,1,0:T(8,128)(2,1)} copy(bf16[1,1,128,8192]{3,2,1,0:T(8,128)(2,1)S(1)} %bitcast.32) | data formatting | bytes 4194304
  84.2 0.8 copy.27
  (1 shorter events, 0.0 us)
Async XLA Ops:
  4.0 1.0 %copy-start.2 = (f32[1,16,8192]{2,1,0:T(8,128)S(1)}, f32[1,16,8192]{2,1,0:T(8,128)}, u32[]{:S(2)}) copy-start(f32[1,16,8192]{2,1,0:T(8,128)} %param.18) | copy-start | bytes 1572868
  5.0 0.9 %copy-start.4 = (f32[1,4,8192]{2,1,0:T(4,128)S(1)}, f32[1,4,8192]{2,1,0:T(4,128)}, u32[]{:S(2)}) copy-start(f32[1,4,8192]{2,1,0:T(4,128)} %param.19) | copy-start | bytes 393220
  5.9 0.8 copy-start.5
  6.7 0.8 copy-start.6
  7.4 70.2 %copy-start.1 = (bf16[1,1,128,2048]{3,2,1,0:T(8,128)(2,1)S(1)}, bf16[1,1,128,2048]{3,2,1,0:T(8,128)(2,1)}, u32[]{:S(2)}) copy-start(bf16[1,1,128,2048]{3,2,1,0:T(8,128)(2,1)} %param.24) | copy-start | bytes 1572868
  7.4 70.2 %copy-start.3 = (bf16[1,1,128,1024]{3,2,1,0:T(8,128)(2,1)S(1)}, bf16[1,1,128,1024]{3,2,1,0:T(8,128)(2,1)}, u32[]{:S(2)}) copy-start(bf16[1,1,128,1024]{3,2,1,0:T(8,128)(2,1)} %param.25) | copy-start | bytes 786436
  77.7 1.2 %copy-start = (bf16[8,8,64,128]{3,2,1,0:T(8,128)(2,1)S(1)}, bf16[8,8,64,128]{3,2,1,0:T(8,128)(2,1)}, u32[]{:S(2)}) copy-start(bf16[8,8,64,128]{3,2,1,0:T(8,128)(2,1)} %get-tuple-element.8.k_ref.v_ref) | copy-start | bytes 3145732
  78.9 4.0 %copy-start.7 = (bf16[128,8192]{1,0:T(8,128)(2,1)S(1)}, bf16[128,8192]{1,0:T(8,128)(2,1)}, u32[]{:S(2)}) copy-start(bf16[128,8192]{1,0:T(8,128)(2,1)} %get-tuple-element.6) | copy-start | bytes 6291460

commit v4 on v3

--- a/solution.py
+++ b/solution.py
@@ -32,6 +32,11 @@
 CHUNKS = 2
 
 
+def silu(v):
+    half = 0.5 * v
+    return half + half * jnp.tanh(half)
+
+
 def mix(i, maps_ref, a_ref, w_ref, skip_ref, x_ref, st_ref, out_ref, last_ref,
         rate_s, gate_s, drive_s, y_s, sig_s, a_s, h_s, u_s):
     tokens = NEW_TOKENS
@@ -51,7 +56,7 @@
             acc = w_ref[0:1, col] * u_s[5 : 5 + tokens, :]
             for k in range(1, KW):
                 acc = acc + w_ref[k : k + 1, col] * u_s[5 + k : 5 + k + tokens, :]
-            signal = acc / (1.0 + jnp.exp(-acc))
+            signal = silu(acc)
             sig_s[:, here : here + LANES] = signal
             rate = rate_s[p, pl.ds(j, tokens, stride=8), :]
             drive_s[q, pl.ds(j, tokens, stride=8), :] = rate * signal
@@ -189,6 +194,20 @@
 
     copies = [push(0, k, ids_ref, ids_all.at[me]) for k in range(1, n)]
     ids_all[me] = ids_ref[...]
+
+    loads[2].wait()
+    loads[3].wait()
+
+    def rates(p, carry):
+        for j in range(GROUPS):
+            col = pl.ds(pl.multiple_of(p * PIECE + j * LANES, LANES), LANES)
+            v = dt_ref[:, col].astype(F32) + bias_ref[:, col]
+            rate = jnp.maximum(v, 0.0) + jnp.log(1.0 + jnp.exp(-jnp.abs(v)))
+            rate_s[p, pl.ds(j, NEW_TOKENS, stride=8), :] = rate
+        return carry
+
+    lax.fori_loop(0, DI // PIECE, rates, 0)
+
     for copy in copies:
         copy.wait()
 
@@ -232,18 +251,18 @@
     st_first = [push(1, k, st_send.at[peer(k)], st_hold.at[me]) for k in range(1, n)]
     st_hold[me] = st_send[me]
 
-    loads[2].wait()
-    loads[3].wait()
-
-    def rates(p, carry):
+    for copy in loads[4:]:
+        copy.wait()
+
+    def gates(p, carry):
         for j in range(GROUPS):
             col = pl.ds(pl.multiple_of(p * PIECE + j * LANES, LANES), LANES)
-            v = dt_ref[:, col].astype(F32) + bias_ref[:, col]
-            rate = jnp.maximum(v, 0.0) + jnp.log1p(jnp.exp(-jnp.abs(v)))
-            rate_s[p, pl.ds(j, NEW_TOKENS, stride=8), :] = rate
+            far = pl.ds(pl.multiple_of(DI + p * PIECE + j * LANES, LANES), LANES)
+            gate = x_ref[:, far].astype(F32)
+            gate_s[:, col] = silu(gate)
         return carry
 
-    lax.fori_loop(0, DI // PIECE, rates, 0)
+    lax.fori_loop(0, DI // PIECE, gates, 0)
 
     for copy in st_first:
         copy.wait()
@@ -261,18 +280,6 @@
     kv_first = [push(2, k, kv_send.at[peer(k)], kv_hold.at[me]) for k in range(1, n)]
     kv_hold[me] = kv_send[me]
 
-    for copy in loads[4:]:
-        copy.wait()
-
-    def gates(p, carry):
-        for j in range(GROUPS):
-            col = pl.ds(pl.multiple_of(p * PIECE + j * LANES, LANES), LANES)
-            far = pl.ds(pl.multiple_of(DI + p * PIECE + j * LANES, LANES), LANES)
-            gate = x_ref[:, far].astype(F32)
-            gate_s[:, col] = gate / (1.0 + jnp.exp(-gate))
-        return carry
-
-    lax.fori_loop(0, DI // PIECE, gates, 0)
     for copy in st_second:
         copy.wait()
 
@@ -328,7 +335,7 @@
     conv = jnp.pad(conv, ((0, 0), (0, 0), (0, 0), (0, 1), (0, 0)))
     conv = conv.reshape(slots, n, CONV_ROWS, LANES)
     vmem = pl.BlockSpec(memory_space=pltpu.VMEM)
-    hbm = pl.BlockSpec(memory_space=pl.ANY)
+    hbm = pl.BlockSpec(memory_space=pltpu.HBM)
     return pl.pallas_call(
         functools.partial(serve_kernel, n),
         out_shape=(
@@ -376,7 +383,7 @@
             pltpu.SemaphoreType.DMA((5, n)),
         ],
         compiler_params=pltpu.CompilerParams(
-            collective_id=0, has_side_effects=True, vmem_limit_bytes=52 * 2**20
+            collective_id=0, has_side_effects=True, vmem_limit_bytes=62 * 2**20
         ),
     )(
         ids,
@@ -423,9 +430,9 @@
             acc = w_ref[0:1, col] * u_s[5 : 5 + tokens, :]
             for k in range(1, KW):
                 acc = acc + w_ref[k : k + 1, col] * u_s[5 + k : 5 + k + tokens, :]
-            signal = acc / (1.0 + jnp.exp(-acc))
+            signal = silu(acc)
             v = dt_ref[:, col].astype(F32) + bias_ref[:, col]
-            rate = jnp.maximum(v, 0.0) + jnp.log1p(jnp.exp(-jnp.abs(v)))
+            rate = jnp.maximum(v, 0.0) + jnp.log(1.0 + jnp.exp(-jnp.abs(v)))
             sig_s[:, col] = signal
             rate_s[q, pl.ds(j, tokens, stride=8), :] = rate
             drive_s[q, pl.ds(j, tokens, stride=8), :] = rate * signal
@@ -463,7 +470,7 @@
             last_ref[:, col] = h_s[q, pl.ds(j, NS, stride=8), :]
             gate = g_ref[:, col].astype(F32)
             y = y_s[q, pl.ds(j, tokens, stride=8), :] + skip_ref[:, col] * sig_s[:, col]
-            out_ref[:, col] = (y * (gate / (1.0 + jnp.exp(-gate)))).astype(BF)
+            out_ref[:, col] = (y * silu(gate)).astype(BF)
 
 
 def mixer(x_gate, dt_raw, state_maps, a_log, conv_weight, dt_bias, d_skip, st):

time: 85.5 us -> 83.2 us (0.973)
  local copies, waits for them, and re-layouts: 9.47 us -> 7.33 us
    unnamed x19 -> x13, local copies, waits for them, and re-layouts: 7.61 us -> 4.23 us
where the time goes in v4:
time: 83.2 us; the launch traced here: 82.9 us
  Pallas kernels  72.9 us (88%)
  local copies, waits for them, and re-layouts  7.33 us (9%)
  between operations  1.98 us (2%)
    pallas_call x1, Pallas kernels, serve(): pl.pallas_call(functools.partial(serve_kernel, n), out_shape=(jax.ShapeDt...  68.9 us
    unnamed x13, local copies, waits for them, and re-layouts  4.23 us
    pallas_call x1, Pallas kernels, attend(): pl.pallas_call(attend_kernel, grid=(1,), out_shape=jax.ShapeDtypeStruct((...  3.97 us

profile of v4, /device:TPU:14, one launch (start us, length us, event | category | flops | bytes accessed | tf_op | source)
XLA Modules:
  0.0 82.9 jit_solution(2643154189894570685)
XLA Ops:
  0.6 1.0 %reshape_squeeze.3 = bf16[2,3,8,8,128]{4,3,2,0,1:T(8,128)(2,1)S(1)} reshape(bf16[1,2,3,8192]{3,1,2,0:T(2,128)(2,1)} %param.23) | data formatting | bytes 196608 | tf_op jit(solution)/shard_map/reshape;squeeze | solution.py:334
  1.6 0.1 copy.21
  1.7 0.7 pad.5
  2.4 0.8 copy.18
  3.2 0.6 bitcast_convert_fusion.maps_ref
  4.5 0.7 concatenate.5
  5.2 0.7 concatenate.6.ids_ref
  5.9 0.0 copy-start.1
  5.9 0.0 copy-start.2
  5.9 68.9 %shard_map.166 = (bf16[128,8192]{1,0:T(8,128)(2,1)}, f32[16,8192]{1,0:T(8,128)}, bf16[8,8,64,128]{3,2,1,0:T(8,128)(2,1)}) custom-call(s32[16,128]{1,0:T(8,128)} %concatenate.6.ids_ref, f32[128,32]{1,0:T(8,128)} %bitcast_convert_fusion.maps_ref, bf16[2,8,32,128]{3,2,1,0:T(8,128)(2,1)} %bitcast.32, f32[2,16,8192]{2,1,0:T(8,128)} %bitcast.30, ...), custom_call_target="tpu_custom_call" | custom-call | tf_op jit(solution)/shard_map/pallas_call | solution.py:339
  75.4 0.0 copy-done.1
  75.5 0.0 copy-done.2
  75.5 0.0 copy-start
  75.5 1.2 %copy-done = bf16[8,8,64,128]{3,2,1,0:T(8,128)(2,1)S(1)} copy-done((bf16[8,8,64,128]{3,2,1,0:T(8,128)(2,1)S(1)}, bf16[8,8,64,128]{3,2,1,0:T(8,128)(2,1)}, u32[]{:S(2)}) %copy-start) | copy-done | bytes 1048600
  76.7 0.0 copy-start.3
  76.7 4.0 %shard_map.167 = bf16[128,2048]{1,0:T(8,128)(2,1)} custom-call(s32[1]{0:T(128)} %bitcast.24.used_ref, bf16[128,2048]{1,0:T(8,128)(2,1)S(1)} %bitcast.25, bf16[128,1024]{1,0:T(8,128)(2,1)S(1)} %bitcast.26, bf16[8,8,64,128]{3,2,1,0:T(8,128)(2,1)S(1)} %copy-done, bf16[8,8,64,128]{3,2,1,0:T(8,128)(2,1)S(1)} %copy-done), custom_call_target="tpu_custom_call" | custom-call | tf_op jit(solution)/shard_map/pallas_call | solution.py:568
  80.7 0.0 copy-done.3
  80.7 0.0 copy-start.4
  80.7 1.3 %copy.26 = bf16[1,1,128,8192]{3,2,1,0:T(8,128)(2,1)} copy(bf16[1,1,128,8192]{3,2,1,0:T(8,128)(2,1)S(1)} %bitcast.28) | data formatting | bytes 4194304
  82.0 0.1 copy-done.4
  82.1 0.8 copy.27
Async XLA Ops:
  5.9 69.6 %copy-start.1 = (bf16[1,1,128,2048]{3,2,1,0:T(8,128)(2,1)S(1)}, bf16[1,1,128,2048]{3,2,1,0:T(8,128)(2,1)}, u32[]{:S(2)}) copy-start(bf16[1,1,128,2048]{3,2,1,0:T(8,128)(2,1)} %param.24) | copy-start | bytes 1572868
  5.9 69.6 %copy-start.2 = (bf16[1,1,128,1024]{3,2,1,0:T(8,128)(2,1)S(1)}, bf16[1,1,128,1024]{3,2,1,0:T(8,128)(2,1)}, u32[]{:S(2)}) copy-start(bf16[1,1,128,1024]{3,2,1,0:T(8,128)(2,1)} %param.25) | copy-start | bytes 786436
  75.5 1.2 %copy-start = (bf16[8,8,64,128]{3,2,1,0:T(8,128)(2,1)S(1)}, bf16[8,8,64,128]{3,2,1,0:T(8,128)(2,1)}, u32[]{:S(2)}) copy-start(bf16[8,8,64,128]{3,2,1,0:T(8,128)(2,1)} %get-tuple-element.8.k_ref.v_ref) | copy-start | bytes 3145732
  76.7 4.0 %copy-start.3 = (bf16[128,8192]{1,0:T(8,128)(2,1)S(1)}, bf16[128,8192]{1,0:T(8,128)(2,1)}, u32[]{:S(2)}) copy-start(bf16[128,8192]{1,0:T(8,128)(2,1)} %get-tuple-element.6) | copy-start | bytes 6291460
  80.7 1.4 %copy-start.4 = (f32[16,8192]{1,0:T(8,128)S(1)}, f32[16,8192]{1,0:T(8,128)}, u32[]{:S(2)}) copy-start(f32[16,8192]{1,0:T(8,128)} %get-tuple-element.7) | copy-start | bytes 1572868
